TPU v7x, 32 devices: a whole 2x2x4 slice. The times are simulated.
32 devices in a mesh: win: 2 (over y), tx: 4 (over z), ty: 4 (over x, core).
Axes of the slice: x: 2, y: 2, z: 4, core: 2. Of those that a mesh axis runs over, the one named last changes fastest.
Arguments:
- dual: float32 [2, 4, 4, 256, 512], P('win', None, None, 'ty', 'tx'), may hold values from -6 to 6
- obs_dual: float32 [2, 2, 256, 512], P('win', None, 'ty', 'tx'), may hold values from -6 to 6
- increment: float32 [2, 4, 4, 256, 512], P('win', None, None, 'ty', 'tx'), may hold values from -6 to 6
- trajectory: float32 [2, 3, 2, 4, 256, 512], P('win', None, None, None, 'ty', 'tx'), may hold values from -0.3 to 0.3
- diffusion: float32 [4, 4], replicated, may hold values from 0.01 to 0.045
- obs_weight: float32 [2, 4, 4], replicated, may hold values from -1.5 to 1.5
- model_var: float32 [2, 4, 4, 256, 512], P('win', None, None, 'ty', 'tx'), may hold values from 0.3 to 3
- obs_var: float32 [2, 2, 256, 512], P('win', None, 'ty', 'tx'), may hold values from 0.5 to 2
Outputs:
- next_dual: float32 [2, 4, 4, 256, 512], P('win', None, None, 'ty', 'tx')
- next_obs: float32 [2, 2, 256, 512], P('win', None, 'ty', 'tx')
- next_increment: float32 [2, 4, 4, 256, 512], P('win', None, None, 'ty', 'tx')
- coeffs: float32 [2], replicated
All inputs are finite; a program needn't handle non-finite values.
Results may differ from a plain program's by a relative error of at most 0.00016.
Values sent between devices are 32-bit elements; how exact they have to be, the bound alone decides.
A program may use at most 128 MiB of HBM per device.

v0:
```python
import jax
import jax.numpy as jnp
from jax import lax
from jax.sharding import PartitionSpec as P


def padded_2(value, sides, width):
    for axis, dim in sides:
        size, length = (lax.axis_size(axis), value.shape[dim])
        up = [(i, (i + 1) % size) for i in range(size)]
        down = [(j, i) for i, j in up]
        last = lax.slice_in_dim(value, length - width, length, axis=dim)
        leading = lax.slice_in_dim(value, 0, width, axis=dim)
        before = lax.ppermute(last, axis, up)
        after = lax.ppermute(leading, axis, down)
        value = jnp.concatenate([before, value, after], axis=dim)
    return value


def from_behind(block, axis, distance):
    devices = range(lax.axis_size(axis))
    route = [(i - distance, i) for i in devices if i - distance in devices]
    return lax.ppermute(block, axis, route)


def prefix(value, axis, combine, identity, reverse):
    size, position = (lax.axis_size(axis), lax.axis_index(axis))
    everything = lax.all_gather(value, axis)
    start = jnp.broadcast_to(jnp.asarray(identity, value.dtype), value.shape)

    def lap(k, before):
        at = size - 1 - k if reverse else k
        reached = at > position if reverse else at < position
        new = combine(before, everything[at])
        return jnp.where(reached, new, before)

    return lax.fori_loop(0, size, lap, start)


def trimmed(padded):
    row_index = lax.axis_index("ty")
    last_row = lax.axis_size("ty") - 1
    rows = padded.shape[-2] - 2
    places = jnp.arange(rows)
    keep_north = jnp.where((places == rows - 1) & (row_index == last_row), 0.0, 1.0).astype(
        padded.dtype
    )[:, None]
    keep_south = jnp.where((places == 0) & (row_index == 0), 0.0, 1.0).astype(padded.dtype)[:, None]
    east = padded[..., 1:-1, 2:]
    west = padded[..., 1:-1, :-2]
    north = padded[..., 2:, 1:-1] * keep_north
    south = padded[..., :-2, 1:-1] * keep_south
    return (east, west, north, south)


def forward_step(field, wind_lon, wind_lat, diffuse):
    pos_lon = jnp.maximum(wind_lon, 0.0)[None]
    neg_lon = jnp.minimum(wind_lon, 0.0)[None]
    pos_lat = jnp.maximum(wind_lat, 0.0)[None]
    neg_lat = jnp.minimum(wind_lat, 0.0)[None]
    padded = padded_2(field, (("tx", 3), ("ty", 2)), 1)
    east, west, north, south = trimmed(padded)
    return (
        field
        - pos_lon * (field - west)
        - neg_lon * (east - field)
        - pos_lat * (field - south)
        - neg_lat * (north - field)
        + diffuse * (east + west + north + south - 4.0 * field)
    )


def back_from_terms(field, wind_lon, wind_lat, diffuse):
    pos_lon = jnp.maximum(wind_lon, 0.0)[None]
    neg_lon = jnp.minimum(wind_lon, 0.0)[None]
    pos_lat = jnp.maximum(wind_lat, 0.0)[None]
    neg_lat = jnp.minimum(wind_lat, 0.0)[None]
    stacked = jnp.stack([field, pos_lon * field, neg_lon * field, pos_lat * field, neg_lat * field])
    padded = padded_2(stacked, (("tx", 4), ("ty", 3)), 1)
    east, west, north, south = trimmed(padded)
    diagonal = 1.0 - pos_lon + neg_lon - pos_lat + neg_lat - 4.0 * diffuse
    return (
        diagonal * field
        + east[1]
        - west[2]
        + north[3]
        - south[4]
        + diffuse * (east[0] + west[0] + north[0] + south[0])
    )


def add_terms(earlier, later):
    return earlier + later


def per_device(dual, obs_dual, increment, trajectory, diffusion, obs_weight, model_var, obs_var):
    multipliers = dual[0]
    observed = obs_dual[0]
    state = increment[0]
    winds = trajectory[0]
    variance = model_var[0]
    obs_variance = obs_var[0]
    diffuse = diffusion[:, :, None, None]
    steps = winds.shape[0]
    following = from_behind(multipliers, "win", -1)
    adjoint_start = (
        jnp.einsum("ofl,oab->flab", obs_weight, observed, precision=lax.Precision.HIGHEST)
        - following
    )
    moved = state
    for index in range(steps):
        moved = forward_step(moved, winds[index, 0], winds[index, 1], diffuse)
    adjoint_field = adjoint_start
    for index in reversed(range(steps)):
        adjoint_field = back_from_terms(adjoint_field, winds[index, 0], winds[index, 1], diffuse)
    carried = from_behind(moved, "win", 1)
    obs_end = jnp.einsum("ofl,flab->oab", obs_weight, moved, precision=lax.Precision.HIGHEST)
    zl = variance * multipliers + state - carried
    zm = obs_variance * observed + obs_end
    zd = multipliers + adjoint_field
    zeros = jnp.zeros_like(zd)
    later_sum = prefix(zd, "win", add_terms, zeros, True)
    new_lam = later_sum + zd
    source = zl - variance * new_lam
    new_state = prefix(source, "win", add_terms, zeros, False) + source
    new_obs = zm / obs_variance
    local_inner = (
        jnp.sum(new_lam * multipliers) + jnp.sum(new_obs * observed) + jnp.sum(new_state * state)
    )
    local_square = (
        jnp.sum(multipliers * multipliers) + jnp.sum(observed * observed) + jnp.sum(state * state)
    )
    inner, square = lax.psum((local_inner, local_square), ("win", "tx", "ty"))
    coeff = inner / square
    rest_lam = new_lam - coeff * multipliers
    rest_obs = new_obs - coeff * observed
    rest_state = new_state - coeff * state
    local_rest = (
        jnp.sum(rest_lam * rest_lam)
        + jnp.sum(rest_obs * rest_obs)
        + jnp.sum(rest_state * rest_state)
    )
    rest_sq = lax.psum(local_rest, ("win", "tx", "ty"))
    count = (
        (multipliers.size * 2 + observed.size)
        * lax.axis_size("win")
        * lax.axis_size("tx")
        * lax.axis_size("ty")
    )
    scale = jnp.sqrt(rest_sq / count + 1e-06)
    return (
        (rest_lam / scale)[None],
        (rest_obs / scale)[None],
        (rest_state / scale)[None],
        jnp.stack([coeff, scale]),
    )


def solution(mesh):
    in_specs = (
        P("win", None, None, "ty", "tx"),
        P("win", None, "ty", "tx"),
        P("win", None, None, "ty", "tx"),
        P("win", None, None, None, "ty", "tx"),
        P(),
        P(),
        P("win", None, None, "ty", "tx"),
        P("win", None, "ty", "tx"),
    )
    out_specs = (
        P("win", None, None, "ty", "tx"),
        P("win", None, "ty", "tx"),
        P("win", None, None, "ty", "tx"),
        P(),
    )
    return jax.shard_map(
        per_device, mesh=mesh, in_specs=in_specs, out_specs=out_specs, check_vma=False
    )
```

profile of v0, /device:TPU:0, one launch (start us, length us, event | category | flops | bytes accessed | tf_op | source)
XLA Modules:
  0.0 334.4 jit_solution(16090004342591973395)
XLA Ops:
  7.2 1.4 copy.153
  8.7 1.3 collective-permute-start
  10.0 1.4 copy.152
  11.4 1.3 fusion.56
  12.6 3.0 collective-permute-start.13
  15.6 2.1 collective-permute-start.14
  19.9 4.9 %collective-permute-done = f32[4,4,64,128]{3,1,2,0:T(4,128)S(1)} collective-permute-done((f32[4,4,64,128]{3,1,2,0:T(4,128)S(1)}, f32[4,4,64,128]{3,1,2,0:T(4,128)S(1)}, u32[]{:S(2)}, u32[]{:S(2)}) %collective-permute-start) | collective-permute-done | bytes 524320 | tf_op jit(solution)/shard_map/ppermute | solution.py:23
  26.5 3.9 %fusion.53 = (f32[5,4,4,64,1]{4,2,3,1,0:T(4,128)}, f32[5,4,4,64,1]{4,2,3,1,0:T(4,128)}) fusion(f32[5,4,4,64,128]{4,2,3,1,0:T(4,128)S(1)} %bitcast_dynamic-update-slice_fusion.10), kind=kLoop, calls=%fused_computation.198 | loop fusion | bytes 81920 | tf_op jit(solution)/shard_map/slice | solution.py:12
  30.5 2.8 copy.52
  33.3 4.4 %collective-permute-start.1 = (f32[5,4,4,64,1]{3,2,4,1,0:T(4,128)}, f32[5,4,4,64,1]{3,2,4,1,0:T(4,128)}, u32[]{:S(2)}, u32[]{:S(2)}) collective-permute-start(f32[5,4,4,64,1]{3,2,4,1,0:T(4,128)} %copy.52), channel_id=1, source_target_pairs={{4,0},{8,4},{12,8},{0,12},{5,1},{9,5},{13,9},{1,13},{6,2},{10,6},{... | collective-permute-start | bytes 61448 | tf_op jit(solution)/shard_map/ppermute | solution.py:15
  37.7 2.8 copy.54
  41.5 2.8 copy.53
  44.2 2.5 collective-permute-done.2
  46.7 2.8 copy.55
  49.6 1.2 pad_maximum_fusion.56
  56.9 4.7 %fusion.5 = (f32[5,4,4,64,128]{4,2,3,1,0:T(4,128)S(1)}, f32[5,4,4,64,128]{4,2,3,1,0:T(4,128)S(1)}) fusion(f32[5,4,4,1,130]{4,2,3,1,0:T(4,128)S(1)} %collective-permute-done.3, f32[5,4,4,64,1]{4,2,3,1,0:T(4,128)S(1)} %copy-done.2, f32[5,4,4,64,128]{4,2,3,1,0:T(4,128)S(1)} %bitcast_dynamic-update-slice_fusion.10, f32[5,4,4,64,1]{4,2,3,1,0:T(4,128)S(1)} %copy-done.3, ...), kind=kLoop, calls=%fused_computation.23 | loop fusion | flops 5242880 | bytes 7988992 | tf_op jit(solution)/shard_map/mul | solution.py:51
  61.6 3.2 bitcast_dynamic-update-slice_fusion.9
  65.8 3.9 %fusion.52 = (f32[5,4,4,64,1]{4,2,3,1,0:T(4,128)}, f32[5,4,4,64,1]{4,2,3,1,0:T(4,128)}) fusion(f32[5,4,4,64,128]{4,2,3,1,0:T(4,128)S(1)} %bitcast_dynamic-update-slice_fusion.5), kind=kLoop, calls=%fused_computation.197 | loop fusion | bytes 81920 | tf_op jit(solution)/shard_map/slice | solution.py:12
  69.7 2.9 copy.62
  73.1 2.8 copy.64
  75.9 1.5 collective-permute-start.6
  77.5 1.5 pad_maximum_fusion.65
  80.7 2.8 copy.63
  83.4 2.8 copy.65
  88.2 3.9 %multiply_add_fusion.2 = f32[4,4,64,128]{3,1,2,0:T(4,128)} fusion(f32[4,4,64,128]{3,1,2,0:T(4,128)S(1)} %bitcast.275, f32[4,4,1,130]{3,1,2,0:T(4,128)} %collective-permute-done.16, f32[4,4,64,1]{3,1,2,0:T(4,128)} %collective-permute-done.14, f32[4,4,64,1]{3,1,2,0:T(4,128)} %collective-permute-done.13, f32[4,4,1,130]{3,1,2,0:T(4,128)} %collective-permute-done.15, ...), kind=kLoop, calls=%fused_computation.144 | loop fusion | flops 3801088 | bytes 1598272 | tf_op jit(solution)/shard_map/add | solution.py:64
  92.3 4.7 %fusion.3 = (f32[5,4,4,64,128]{4,2,3,1,0:T(4,128)S(1)}, f32[5,4,4,64,128]{4,2,3,1,0:T(4,128)S(1)}) fusion(f32[5,4,4,1,130]{4,2,3,1,0:T(4,128)S(1)} %collective-permute-done.7, f32[5,4,4,64,1]{4,2,3,1,0:T(4,128)S(1)} %copy-done.5, f32[5,4,4,64,128]{4,2,3,1,0:T(4,128)S(1)} %bitcast_dynamic-update-slice_fusion.5, f32[5,4,4,64,1]{4,2,3,1,0:T(4,128)S(1)} %copy-done.7, ...), kind=kLoop, calls=%fused_computation.15 | loop fusion | flops 5242880 | bytes 7988992 | tf_op jit(solution)/shard_map/mul | solution.py:51
  97.1 3.2 bitcast_dynamic-update-slice_fusion.4
  101.3 3.9 %fusion.51 = (f32[5,4,4,64,1]{4,2,3,1,0:T(4,128)}, f32[5,4,4,64,1]{4,2,3,1,0:T(4,128)}) fusion(f32[5,4,4,64,128]{4,2,3,1,0:T(4,128)S(1)} %bitcast_dynamic-update-slice_fusion), kind=kLoop, calls=%fused_computation.196 | loop fusion | bytes 81920 | tf_op jit(solution)/shard_map/slice | solution.py:12
  105.2 2.9 copy.72
  108.1 2.3 collective-permute-start.9
  110.4 2.8 copy.74
  113.2 1.3 fusion.55
  114.4 3.8 %collective-permute-start.18 = (f32[4,4,64,1]{3,1,2,0:T(4,128)}, f32[4,4,64,1]{3,1,2,0:T(4,128)}, u32[]{:S(2)}, u32[]{:S(2)}) collective-permute-start(f32[4,4,64,1]{3,1,2,0:T(4,128)} %get-tuple-element.315), channel_id=1, source_target_pairs={{4,0},{8,4},{12,8},{0,12},{5,1},{9,5},{13,9},{1,13},{6,2},{10,6},{... | collective-permute-start | bytes 12296 | tf_op jit(solution)/shard_map/ppermute | solution.py:15
  118.2 2.8 copy.73
  121.0 2.8 copy.75
  125.5 5.9 %collective-permute-done.17 = f32[4,4,64,1]{3,1,2,0:T(4,128)} collective-permute-done((f32[4,4,64,1]{3,1,2,0:T(4,128)}, f32[4,4,64,1]{3,1,2,0:T(4,128)}, u32[]{:S(2)}, u32[]{:S(2)}) %collective-permute-start.17) | collective-permute-done | bytes 4128 | tf_op jit(solution)/shard_map/ppermute | solution.py:14
  131.4 10.1 %collective-permute-done.18 = f32[4,4,64,1]{3,1,2,0:T(4,128)} collective-permute-done((f32[4,4,64,1]{3,1,2,0:T(4,128)}, f32[4,4,64,1]{3,1,2,0:T(4,128)}, u32[]{:S(2)}, u32[]{:S(2)}) %collective-permute-start.18) | collective-permute-done | bytes 4128 | tf_op jit(solution)/shard_map/ppermute | solution.py:15
  141.4 1.5 pad_maximum_fusion.62
  142.9 1.9 collective-permute-start.20
  144.9 4.7 %fusion.1 = (f32[5,4,4,64,128]{4,2,3,1,0:T(4,128)S(1)}, f32[5,4,4,64,128]{4,2,3,1,0:T(4,128)S(1)}) fusion(f32[5,4,4,1,130]{4,2,3,1,0:T(4,128)S(1)} %collective-permute-done.11, f32[5,4,4,64,1]{4,2,3,1,0:T(4,128)S(1)} %copy-done.4, f32[5,4,4,64,128]{4,2,3,1,0:T(4,128)S(1)} %bitcast_dynamic-update-slice_fusion, f32[5,4,4,64,1]{4,2,3,1,0:T(4,128)S(1)} %copy-done.6, ...), kind=kLoop, calls=%fused_computation.7 | loop fusion | flops 5242880 | bytes 7988992 | tf_op jit(solution)/shard_map/mul | solution.py:51
  149.6 1.8 fusion.17
  153.2 4.0 %multiply_add_fusion.1 = f32[4,4,64,128]{3,1,2,0:T(4,128)S(1)} fusion(f32[4,4,64,128]{3,1,2,0:T(4,128)} %multiply_add_fusion.2, f32[4,4,1,130]{3,1,2,0:T(4,128)} %collective-permute-done.20, f32[4,4,64,1]{3,1,2,0:T(4,128)} %collective-permute-done.18, f32[4,4,64,1]{3,1,2,0:T(4,128)} %collective-permute-done.17, ...), kind=kLoop, calls=%fused_computation.143 | loop fusion | flops 3801088 | bytes 1598272 | tf_op jit(solution)/shard_map/add | solution.py:64
  157.5 1.5 collective-permute-start.21
  159.0 2.3 collective-permute-start.22
  161.4 12.8 %collective-permute-done.21 = f32[4,4,64,1]{3,1,2,0:T(4,128)S(1)} collective-permute-done((f32[4,4,64,1]{3,1,2,0:T(4,128)S(1)}, f32[4,4,64,1]{3,1,2,0:T(4,128)S(1)}, u32[]{:S(2)}, u32[]{:S(2)}) %collective-permute-start.21) | collective-permute-done | bytes 4128 | tf_op jit(solution)/shard_map/ppermute | solution.py:14
  174.2 8.7 %collective-permute-done.22 = f32[4,4,64,1]{3,1,2,0:T(4,128)S(1)} collective-permute-done((f32[4,4,64,1]{3,1,2,0:T(4,128)S(1)}, f32[4,4,64,1]{3,1,2,0:T(4,128)S(1)}, u32[]{:S(2)}, u32[]{:S(2)}) %collective-permute-start.22) | collective-permute-done | bytes 4128 | tf_op jit(solution)/shard_map/ppermute | solution.py:15
  183.1 1.7 collective-permute-start.24
  184.8 1.4 collective-permute-done.23
  186.3 2.0 multiply_add_fusion
  188.3 4.1 %collective-permute-start.25 = (f32[4,4,64,128]{3,1,2,0:T(4,128)S(1)}, f32[4,4,64,128]{3,1,2,0:T(4,128)S(1)}, u32[]{:S(2)}, u32[]{:S(2)}) collective-permute-start(f32[4,4,64,128]{3,1,2,0:T(4,128)S(1)} %multiply_add_fusion), channel_id=1, source_target_pairs={{0,16},{1,17},{2,18},{3,19},{4,20},{5,21},{6,22},{7,23},{8,24},{9,... | collective-permute-start | bytes 1572872 | tf_op jit(solution)/shard_map/ppermute | solution.py:23
  192.4 2.6 while.30
  192.5 1.3 add_select_fusion.4
  193.8 1.2 add_select_fusion.4
  195.0 9.3 %collective-permute-done.25 = f32[4,4,64,128]{3,1,2,0:T(4,128)S(1)} collective-permute-done((f32[4,4,64,128]{3,1,2,0:T(4,128)S(1)}, f32[4,4,64,128]{3,1,2,0:T(4,128)S(1)}, u32[]{:S(2)}, u32[]{:S(2)}) %collective-permute-start.25) | collective-permute-done | bytes 524320 | tf_op jit(solution)/shard_map/ppermute | solution.py:23
  205.1 2.7 fusion.41
  208.8 2.3 fusion.45
  214.9 16.0 %all-gather.7.cloned.1.call-done = f32[8,4,64,128]{3,2,1,0:T(8,128)} async-done(((f32[4,4,64,128]{3,2,1,0:T(8,128)}), f32[8,4,64,128]{3,2,1,0:T(8,128)}) %all-gather.7.cloned.1.call-update) | async-done | bytes 1048592 | tf_op jit(solution)/shard_map/all_gather | solution.py:28
  230.9 2.5 while.31
  230.9 1.2 add_select_fusion.5
  232.1 1.2 add_select_fusion.5
  233.4 1.4 multiply_reduce_fusion.2
  236.1 39.6 %all-reduce = (f32[]{:T(128)}, f32[]{:T(128)}) all-reduce(f32[]{:T(128)S(6)} %add.308, f32[]{:T(128)S(6)} %add.310), channel_id=1, replica_groups=mesh['win'=2,'tx'=4,'ty'=4] {'win','tx','ty'}, use_global_device_ids=true, to_apply=%region_7.8 | all-reduce | flops 2 | bytes 16 | tf_op jit(solution)/shard_map/psum | solution.py:133
  277.0 1.3 multiply_reduce_fusion
  281.9 41.2 %psum.23 = f32[]{:T(128)} all-reduce(f32[]{:T(128)S(6)} %add.312), channel_id=1, replica_groups=mesh['win'=2,'tx'=4,'ty'=4] {'win','tx','ty'}, use_global_device_ids=true, to_apply=%region_15.16 | all-reduce | flops 1 | bytes 8 | tf_op jit(solution)/shard_map/psum | solution.py:143
  (189 shorter events, 28.9 us)
Async XLA Ops:
  7.2 10.6 %copy-start.19 = (f32[1,3,2,4,64,128]{5,4,3,2,1,0:T(8,128)S(1)}, f32[1,3,2,4,64,128]{5,4,3,2,1,0:T(8,128)}, u32[]{:S(2)}) copy-start(f32[1,3,2,4,64,128]{5,4,3,2,1,0:T(8,128)} %param.15) | copy-start | bytes 2359300
  7.2 185.2 %all-gather.5.cloned.1.call-start = ((), (), s32[]{:S(2)}) async-start(), calls=%async_computation | async-start | bytes 1572864 | tf_op jit(solution)/shard_map/all_gather | solution.py:28
  8.7 16.2 %collective-permute-start = (f32[4,4,64,128]{3,1,2,0:T(4,128)S(1)}, f32[4,4,64,128]{3,1,2,0:T(4,128)S(1)}, u32[]{:S(2)}, u32[]{:S(2)}) collective-permute-start(f32[4,4,64,128]{3,1,2,0:T(4,128)S(1)} %bitcast.280), channel_id=1, source_target_pairs={{16,0},{17,1},{18,2},{19,3},{20,4},{21,5},{22,6},{23,7},{24,8},{25... | collective-permute-start | bytes 1572872 | tf_op jit(solution)/shard_map/ppermute | solution.py:23
  11.4 7.7 %copy-start.13 = (f32[1,4,4,64,128]{4,2,3,1,0:T(4,128)}, f32[1,4,4,64,128]{4,2,3,1,0:T(4,128)S(1)}, u32[]{:S(2)}) copy-start(f32[1,4,4,64,128]{4,2,3,1,0:T(4,128)S(1)} %copy.152) | copy-start | bytes 1572868
  12.6 12.2 %copy-start.30 = (f32[1,2,64,128]{3,2,1,0:T(8,128)S(1)}, f32[1,2,64,128]{3,2,1,0:T(8,128)}, u32[]{:S(2)}) copy-start(f32[1,2,64,128]{3,2,1,0:T(8,128)} %param.13) | copy-start | bytes 196612
  12.6 12.2 %copy-start.48 = (f32[2,4,4]{2,1,0:T(4,128)S(1)}, f32[2,4,4]{2,1,0:T(4,128)}, u32[]{:S(2)}) copy-start(f32[2,4,4]{2,1,0:T(4,128)} %param.17) | copy-start | bytes 388
  12.6 64.8 %collective-permute-start.13 = (f32[4,4,64,1]{3,1,2,0:T(4,128)}, f32[4,4,64,1]{3,1,2,0:T(4,128)}, u32[]{:S(2)}, u32[]{:S(2)}) collective-permute-start(f32[4,4,64,1]{3,1,2,0:T(4,128)} %get-tuple-element.316), channel_id=1, source_target_pairs={{0,4},{4,8},{8,12},{12,0},{1,5},{5,9},{9,13},{13,1},{2,6},{6,10},{... | collective-permute-start | bytes 12296 | tf_op jit(solution)/shard_map/ppermute | solution.py:14
  15.6 61.8 %collective-permute-start.14 = (f32[4,4,64,1]{3,1,2,0:T(4,128)}, f32[4,4,64,1]{3,1,2,0:T(4,128)}, u32[]{:S(2)}, u32[]{:S(2)}) collective-permute-start(f32[4,4,64,1]{3,1,2,0:T(4,128)} %get-tuple-element.317), channel_id=1, source_target_pairs={{4,0},{8,4},{12,8},{0,12},{5,1},{9,5},{13,9},{1,13},{6,2},{10,6},{... | collective-permute-start | bytes 12296 | tf_op jit(solution)/shard_map/ppermute | solution.py:15
  19.2 7.2 %copy-start.20 = (f32[4,64,128]{2,0,1:T(4,128)}, f32[4,64,128]{2,0,1:T(4,128)S(1)}, u32[]{:S(2)}) copy-start(f32[4,64,128]{2,0,1:T(4,128)S(1)} %copy.51) | copy-start | bytes 393220
  26.5 30.3 %copy-start.1 = (f32[5,4,4,64,128]{4,2,3,1,0:T(4,128)}, f32[5,4,4,64,128]{4,2,3,1,0:T(4,128)S(1)}, u32[]{:S(2)}) copy-start(f32[5,4,4,64,128]{4,2,3,1,0:T(4,128)S(1)} %bitcast_dynamic-update-slice_fusion.10) | copy-start | bytes 7864324
  30.5 10.1 %copy-start.47 = (f32[4,4]{1,0:T(4,128)S(1)}, f32[4,4]{1,0:T(4,128)}, u32[]{:S(2)}) copy-start(f32[4,4]{1,0:T(4,128)} %param.16) | copy-start | bytes 196
  33.3 8.2 %collective-permute-start.1 = (f32[5,4,4,64,1]{3,2,4,1,0:T(4,128)}, f32[5,4,4,64,1]{3,2,4,1,0:T(4,128)}, u32[]{:S(2)}, u32[]{:S(2)}) collective-permute-start(f32[5,4,4,64,1]{3,2,4,1,0:T(4,128)} %copy.52), channel_id=1, source_target_pairs={{4,0},{8,4},{12,8},{0,12},{5,1},{9,5},{13,9},{1,13},{6,2},{10,6},{... | collective-permute-start | bytes 61448 | tf_op jit(solution)/shard_map/ppermute | solution.py:15
  40.6 6.1 %collective-permute-start.2 = (f32[5,4,4,64,1]{3,2,4,1,0:T(4,128)}, f32[5,4,4,64,1]{3,2,4,1,0:T(4,128)}, u32[]{:S(2)}, u32[]{:S(2)}) collective-permute-start(f32[5,4,4,64,1]{3,2,4,1,0:T(4,128)} %copy.54), channel_id=1, source_target_pairs={{0,4},{4,8},{8,12},{12,0},{1,5},{5,9},{9,13},{13,1},{2,6},{6,10},{... | collective-permute-start | bytes 61448 | tf_op jit(solution)/shard_map/ppermute | solution.py:14
  49.5 4.4 %copy-start.36 = (f32[4,64,128]{2,1,0:T(8,128)S(1)}, f32[4,64,128]{2,1,0:T(8,128)}, u32[]{:S(2)}) copy-start(f32[4,64,128]{2,1,0:T(8,128)} %get-tuple-element.301) | copy-start | bytes 393220
  49.5 5.1 %copy-start.35 = (f32[4,64,128]{2,1,0:T(8,128)S(1)}, f32[4,64,128]{2,1,0:T(8,128)}, u32[]{:S(2)}) copy-start(f32[4,64,128]{2,1,0:T(8,128)} %get-tuple-element.310) | copy-start | bytes 393220
  49.5 5.8 %copy-start.34 = (f32[4,64,128]{2,1,0:T(8,128)S(1)}, f32[4,64,128]{2,1,0:T(8,128)}, u32[]{:S(2)}) copy-start(f32[4,64,128]{2,1,0:T(8,128)} %get-tuple-element.302) | copy-start | bytes 393220
  49.6 6.6 %copy-start.42 = (f32[4,64,128]{2,1,0:T(8,128)S(1)}, f32[4,64,128]{2,1,0:T(8,128)}, u32[]{:S(2)}) copy-start(f32[4,64,128]{2,1,0:T(8,128)} %get-tuple-element.297) | copy-start | bytes 393220
  49.6 7.3 %copy-start.3 = (f32[5,4,4,64,1]{4,2,3,1,0:T(4,128)S(1)}, f32[5,4,4,64,1]{4,2,3,1,0:T(4,128)}, u32[]{:S(2)}) copy-start(f32[5,4,4,64,1]{4,2,3,1,0:T(4,128)} %copy.55) | copy-start | bytes 61444
  50.8 6.1 %copy-start.2 = (f32[5,4,4,64,1]{4,2,3,1,0:T(4,128)S(1)}, f32[5,4,4,64,1]{4,2,3,1,0:T(4,128)}, u32[]{:S(2)}) copy-start(f32[5,4,4,64,1]{4,2,3,1,0:T(4,128)} %copy.53) | copy-start | bytes 61444
  50.8 6.1 %collective-permute-start.3 = (f32[5,4,4,1,130]{4,2,3,1,0:T(4,128)S(1)}, f32[5,4,4,1,130]{4,2,3,1,0:T(4,128)S(1)}, u32[]{:S(2)}, u32[]{:S(2)}) collective-permute-start(f32[5,4,4,1,130]{4,2,3,1,0:T(4,128)S(1)} %get-tuple-element.283), channel_id=1, source_target_pairs={{1,0},{2,1},{3,2},{0,3},{5,4},{6,5},{7,6},{4,7},{9,8},{10,9},{11,1... | collective-permute-start | bytes 124808 | tf_op jit(solution)/shard_map/ppermute | solution.py:15
  50.8 6.0 %collective-permute-start.4 = (f32[5,4,4,1,130]{4,2,3,1,0:T(4,128)S(1)}, f32[5,4,4,1,130]{4,2,3,1,0:T(4,128)S(1)}, u32[]{:S(2)}, u32[]{:S(2)}) collective-permute-start(f32[5,4,4,1,130]{4,2,3,1,0:T(4,128)S(1)} %get-tuple-element.284), channel_id=1, source_target_pairs={{0,1},{1,2},{2,3},{3,0},{4,5},{5,6},{6,7},{7,4},{8,9},{9,10},{10,1... | collective-permute-start | bytes 124808 | tf_op jit(solution)/shard_map/ppermute | solution.py:14
  52.0 12.8 %copy-start.22 = (f32[4,64,128]{2,0,1:T(4,128)}, f32[4,64,128]{2,0,1:T(4,128)S(1)}, u32[]{:S(2)}) copy-start(f32[4,64,128]{2,0,1:T(4,128)S(1)} %copy.58) | copy-start | bytes 393220
  52.2 12.9 %copy-start.23 = (f32[4,64,128]{2,0,1:T(4,128)}, f32[4,64,128]{2,0,1:T(4,128)S(1)}, u32[]{:S(2)}) copy-start(f32[4,64,128]{2,0,1:T(4,128)S(1)} %copy.59) | copy-start | bytes 393220
  52.3 12.9 %copy-start.24 = (f32[4,64,128]{2,0,1:T(4,128)}, f32[4,64,128]{2,0,1:T(4,128)S(1)}, u32[]{:S(2)}) copy-start(f32[4,64,128]{2,0,1:T(4,128)S(1)} %copy.60) | copy-start | bytes 393220
  52.4 12.9 %copy-start.25 = (f32[4,64,128]{2,0,1:T(4,128)}, f32[4,64,128]{2,0,1:T(4,128)S(1)}, u32[]{:S(2)}) copy-start(f32[4,64,128]{2,0,1:T(4,128)S(1)} %copy.61) | copy-start | bytes 393220
  65.8 26.5 %copy-start = (f32[5,4,4,64,128]{4,2,3,1,0:T(4,128)}, f32[5,4,4,64,128]{4,2,3,1,0:T(4,128)S(1)}, u32[]{:S(2)}) copy-start(f32[5,4,4,64,128]{4,2,3,1,0:T(4,128)S(1)} %bitcast_dynamic-update-slice_fusion.5) | copy-start | bytes 7864324
  69.7 7.7 %copy-start.14 = (f32[1,4,4,64,128]{4,2,3,1,0:T(4,128)S(1)}, f32[1,4,4,64,128]{4,2,3,1,0:T(4,128)}, u32[]{:S(2)}) copy-start(f32[1,4,4,64,128]{4,2,3,1,0:T(4,128)} %copy-done.13) | copy-start | bytes 1572868
  72.6 8.1 %collective-permute-start.5 = (f32[5,4,4,64,1]{3,2,4,1,0:T(4,128)}, f32[5,4,4,64,1]{3,2,4,1,0:T(4,128)}, u32[]{:S(2)}, u32[]{:S(2)}) collective-permute-start(f32[5,4,4,64,1]{3,2,4,1,0:T(4,128)} %copy.62), channel_id=1, source_target_pairs={{4,0},{8,4},{12,8},{0,12},{5,1},{9,5},{13,9},{1,13},{6,2},{10,6},{... | collective-permute-start | bytes 61448 | tf_op jit(solution)/shard_map/ppermute | solution.py:15
  75.9 7.5 %collective-permute-start.6 = (f32[5,4,4,64,1]{3,2,4,1,0:T(4,128)}, f32[5,4,4,64,1]{3,2,4,1,0:T(4,128)}, u32[]{:S(2)}, u32[]{:S(2)}) collective-permute-start(f32[5,4,4,64,1]{3,2,4,1,0:T(4,128)} %copy.64), channel_id=1, source_target_pairs={{0,4},{4,8},{8,12},{12,0},{1,5},{5,9},{9,13},{13,1},{2,6},{6,10},{... | collective-permute-start | bytes 61448 | tf_op jit(solution)/shard_map/ppermute | solution.py:14
  78.9 9.2 %collective-permute-start.15 = (f32[4,4,1,130]{3,1,2,0:T(4,128)}, f32[4,4,1,130]{3,1,2,0:T(4,128)}, u32[]{:S(2)}, u32[]{:S(2)}) collective-permute-start(f32[4,4,1,130]{3,1,2,0:T(4,128)} %get-tuple-element.295), channel_id=1, source_target_pairs={{0,1},{1,2},{2,3},{3,0},{4,5},{5,6},{6,7},{7,4},{8,9},{9,10},{10,1... | collective-permute-start | bytes 24968 | tf_op jit(solution)/shard_map/ppermute | solution.py:14
  79.6 8.6 %collective-permute-start.16 = (f32[4,4,1,130]{3,1,2,0:T(4,128)}, f32[4,4,1,130]{3,1,2,0:T(4,128)}, u32[]{:S(2)}, u32[]{:S(2)}) collective-permute-start(f32[4,4,1,130]{3,1,2,0:T(4,128)} %get-tuple-element.296), channel_id=1, source_target_pairs={{1,0},{2,1},{3,2},{0,3},{5,4},{6,5},{7,6},{4,7},{9,8},{10,9},{11,1... | collective-permute-start | bytes 24968 | tf_op jit(solution)/shard_map/ppermute | solution.py:15
  86.3 6.1 %copy-start.7 = (f32[5,4,4,64,1]{4,2,3,1,0:T(4,128)S(1)}, f32[5,4,4,64,1]{4,2,3,1,0:T(4,128)}, u32[]{:S(2)}) copy-start(f32[5,4,4,64,1]{4,2,3,1,0:T(4,128)} %copy.65) | copy-start | bytes 61444
  87.5 4.9 %copy-start.5 = (f32[5,4,4,64,1]{4,2,3,1,0:T(4,128)S(1)}, f32[5,4,4,64,1]{4,2,3,1,0:T(4,128)}, u32[]{:S(2)}) copy-start(f32[5,4,4,64,1]{4,2,3,1,0:T(4,128)} %copy.63) | copy-start | bytes 61444
  87.5 4.7 %collective-permute-start.7 = (f32[5,4,4,1,130]{4,2,3,1,0:T(4,128)S(1)}, f32[5,4,4,1,130]{4,2,3,1,0:T(4,128)S(1)}, u32[]{:S(2)}, u32[]{:S(2)}) collective-permute-start(f32[5,4,4,1,130]{4,2,3,1,0:T(4,128)S(1)} %get-tuple-element.279), channel_id=1, source_target_pairs={{1,0},{2,1},{3,2},{0,3},{5,4},{6,5},{7,6},{4,7},{9,8},{10,9},{11,1... | collective-permute-start | bytes 124808 | tf_op jit(solution)/shard_map/ppermute | solution.py:15
  87.5 4.8 %collective-permute-start.8 = (f32[5,4,4,1,130]{4,2,3,1,0:T(4,128)S(1)}, f32[5,4,4,1,130]{4,2,3,1,0:T(4,128)S(1)}, u32[]{:S(2)}, u32[]{:S(2)}) collective-permute-start(f32[5,4,4,1,130]{4,2,3,1,0:T(4,128)S(1)} %get-tuple-element.280), channel_id=1, source_target_pairs={{0,1},{1,2},{2,3},{3,0},{4,5},{5,6},{6,7},{7,4},{8,9},{9,10},{10,1... | collective-permute-start | bytes 124808 | tf_op jit(solution)/shard_map/ppermute | solution.py:14
  92.1 4.9 %copy-start.12 = (f32[4,4,64,128]{3,1,2,0:T(4,128)S(1)}, f32[4,4,64,128]{3,1,2,0:T(4,128)}, u32[]{:S(2)}) copy-start(f32[4,4,64,128]{3,1,2,0:T(4,128)} %copy-done.11) | copy-start | bytes 1572868
  92.1 4.9 %copy-start.33 = (f32[4,64,128]{2,0,1:T(4,128)S(1)}, f32[4,64,128]{2,0,1:T(4,128)}, u32[]{:S(2)}) copy-start(f32[4,64,128]{2,0,1:T(4,128)} %copy.44) | copy-start | bytes 393220
  105.2 8.0 %copy-start.15 = (f32[4,4,64,128]{3,1,2,0:T(4,128)S(1)}, f32[4,4,64,128]{3,1,2,0:T(4,128)}, u32[]{:S(2)}) copy-start(f32[4,4,64,128]{3,1,2,0:T(4,128)} %multiply_add_fusion.2) | copy-start | bytes 1572868
  108.1 10.2 %collective-permute-start.9 = (f32[5,4,4,64,1]{3,2,4,1,0:T(4,128)}, f32[5,4,4,64,1]{3,2,4,1,0:T(4,128)}, u32[]{:S(2)}, u32[]{:S(2)}) collective-permute-start(f32[5,4,4,64,1]{3,2,4,1,0:T(4,128)} %copy.72), channel_id=1, source_target_pairs={{4,0},{8,4},{12,8},{0,12},{5,1},{9,5},{13,9},{1,13},{6,2},{10,6},{... | collective-permute-start | bytes 61448 | tf_op jit(solution)/shard_map/ppermute | solution.py:15
  113.2 7.9 %collective-permute-start.10 = (f32[5,4,4,64,1]{3,2,4,1,0:T(4,128)}, f32[5,4,4,64,1]{3,2,4,1,0:T(4,128)}, u32[]{:S(2)}, u32[]{:S(2)}) collective-permute-start(f32[5,4,4,64,1]{3,2,4,1,0:T(4,128)} %copy.74), channel_id=1, source_target_pairs={{0,4},{4,8},{8,12},{12,0},{1,5},{5,9},{9,13},{13,1},{2,6},{6,10},{... | collective-permute-start | bytes 61448 | tf_op jit(solution)/shard_map/ppermute | solution.py:14
  114.4 17.0 %collective-permute-start.17 = (f32[4,4,64,1]{3,1,2,0:T(4,128)}, f32[4,4,64,1]{3,1,2,0:T(4,128)}, u32[]{:S(2)}, u32[]{:S(2)}) collective-permute-start(f32[4,4,64,1]{3,1,2,0:T(4,128)} %get-tuple-element.314), channel_id=1, source_target_pairs={{0,4},{4,8},{8,12},{12,0},{1,5},{5,9},{9,13},{13,1},{2,6},{6,10},{... | collective-permute-start | bytes 12296 | tf_op jit(solution)/shard_map/ppermute | solution.py:14
  114.4 27.0 %collective-permute-start.18 = (f32[4,4,64,1]{3,1,2,0:T(4,128)}, f32[4,4,64,1]{3,1,2,0:T(4,128)}, u32[]{:S(2)}, u32[]{:S(2)}) collective-permute-start(f32[4,4,64,1]{3,1,2,0:T(4,128)} %get-tuple-element.315), channel_id=1, source_target_pairs={{4,0},{8,4},{12,8},{0,12},{5,1},{9,5},{13,9},{1,13},{6,2},{10,6},{... | collective-permute-start | bytes 12296 | tf_op jit(solution)/shard_map/ppermute | solution.py:15
  123.8 21.1 %copy-start.4 = (f32[5,4,4,64,1]{4,2,3,1,0:T(4,128)S(1)}, f32[5,4,4,64,1]{4,2,3,1,0:T(4,128)}, u32[]{:S(2)}) copy-start(f32[5,4,4,64,1]{4,2,3,1,0:T(4,128)} %copy.73) | copy-start | bytes 61444
  123.8 21.1 %copy-start.6 = (f32[5,4,4,64,1]{4,2,3,1,0:T(4,128)S(1)}, f32[5,4,4,64,1]{4,2,3,1,0:T(4,128)}, u32[]{:S(2)}) copy-start(f32[5,4,4,64,1]{4,2,3,1,0:T(4,128)} %copy.75) | copy-start | bytes 61444
  125.0 19.9 %collective-permute-start.11 = (f32[5,4,4,1,130]{4,2,3,1,0:T(4,128)S(1)}, f32[5,4,4,1,130]{4,2,3,1,0:T(4,128)S(1)}, u32[]{:S(2)}, u32[]{:S(2)}) collective-permute-start(f32[5,4,4,1,130]{4,2,3,1,0:T(4,128)S(1)} %get-tuple-element.275), channel_id=1, source_target_pairs={{1,0},{2,1},{3,2},{0,3},{5,4},{6,5},{7,6},{4,7},{9,8},{10,9},{11,1... | collective-permute-start | bytes 124808 | tf_op jit(solution)/shard_map/ppermute | solution.py:15
  125.4 19.5 %collective-permute-start.12 = (f32[5,4,4,1,130]{4,2,3,1,0:T(4,128)S(1)}, f32[5,4,4,1,130]{4,2,3,1,0:T(4,128)S(1)}, u32[]{:S(2)}, u32[]{:S(2)}) collective-permute-start(f32[5,4,4,1,130]{4,2,3,1,0:T(4,128)S(1)} %get-tuple-element.276), channel_id=1, source_target_pairs={{0,1},{1,2},{2,3},{3,0},{4,5},{5,6},{6,7},{7,4},{8,9},{9,10},{10,1... | collective-permute-start | bytes 124808 | tf_op jit(solution)/shard_map/ppermute | solution.py:14
  142.9 10.3 %collective-permute-start.19 = (f32[4,4,1,130]{3,1,2,0:T(4,128)}, f32[4,4,1,130]{3,1,2,0:T(4,128)}, u32[]{:S(2)}, u32[]{:S(2)}) collective-permute-start(f32[4,4,1,130]{3,1,2,0:T(4,128)} %get-tuple-element.293), channel_id=1, source_target_pairs={{0,1},{1,2},{2,3},{3,0},{4,5},{5,6},{6,7},{7,4},{8,9},{9,10},{10,1... | collective-permute-start | bytes 24968 | tf_op jit(solution)/shard_map/ppermute | solution.py:14
  142.9 6.7 %copy-start.8 = (f32[1,4,4,64,128]{4,3,2,1,0:T(8,128)S(1)}, f32[1,4,4,64,128]{4,3,2,1,0:T(8,128)}, u32[]{:S(2)}) copy-start(f32[1,4,4,64,128]{4,3,2,1,0:T(8,128)} %param.12) | copy-start | bytes 1572868
  142.9 6.7 %copy-start.10 = (f32[4,4,64,128]{3,1,2,0:T(4,128)S(1)}, f32[4,4,64,128]{3,1,2,0:T(4,128)}, u32[]{:S(2)}) copy-start(f32[4,4,64,128]{3,1,2,0:T(4,128)} %copy-done.9) | copy-start | bytes 1572868
  142.9 6.7 %copy-start.32 = (f32[4,64,128]{2,0,1:T(4,128)S(1)}, f32[4,64,128]{2,0,1:T(4,128)}, u32[]{:S(2)}) copy-start(f32[4,64,128]{2,0,1:T(4,128)} %copy.43) | copy-start | bytes 393220
  142.9 10.3 %collective-permute-start.20 = (f32[4,4,1,130]{3,1,2,0:T(4,128)}, f32[4,4,1,130]{3,1,2,0:T(4,128)}, u32[]{:S(2)}, u32[]{:S(2)}) collective-permute-start(f32[4,4,1,130]{3,1,2,0:T(4,128)} %get-tuple-element.294), channel_id=1, source_target_pairs={{1,0},{2,1},{3,2},{0,3},{5,4},{6,5},{7,6},{4,7},{9,8},{10,9},{11,1... | collective-permute-start | bytes 24968 | tf_op jit(solution)/shard_map/ppermute | solution.py:15
  153.1 33.2 %copy-start.21 = (f32[4,64,128]{2,0,1:T(4,128)S(1)}, f32[4,64,128]{2,0,1:T(4,128)}, u32[]{:S(2)}) copy-start(f32[4,64,128]{2,0,1:T(4,128)} %copy-done.20) | copy-start | bytes 393220
  153.1 77.8 %all-gather.7.cloned.1.call-start = ((), (), s32[]{:S(2)}) async-start(), calls=%async_computation.1 | async-start | bytes 1572864 | tf_op jit(solution)/shard_map/all_gather | solution.py:28
  157.5 16.7 %collective-permute-start.21 = (f32[4,4,64,1]{3,1,2,0:T(4,128)S(1)}, f32[4,4,64,1]{3,1,2,0:T(4,128)S(1)}, u32[]{:S(2)}, u32[]{:S(2)}) collective-permute-start(f32[4,4,64,1]{3,1,2,0:T(4,128)S(1)} %get-tuple-element.312), channel_id=1, source_target_pairs={{0,4},{4,8},{8,12},{12,0},{1,5},{5,9},{9,13},{13,1},{2,6},{6,10},{... | collective-permute-start | bytes 12296 | tf_op jit(solution)/shard_map/ppermute | solution.py:14
  159.0 23.9 %collective-permute-start.22 = (f32[4,4,64,1]{3,1,2,0:T(4,128)S(1)}, f32[4,4,64,1]{3,1,2,0:T(4,128)S(1)}, u32[]{:S(2)}, u32[]{:S(2)}) collective-permute-start(f32[4,4,64,1]{3,1,2,0:T(4,128)S(1)} %get-tuple-element.313), channel_id=1, source_target_pairs={{4,0},{8,4},{12,8},{0,12},{5,1},{9,5},{13,9},{1,13},{6,2},{10,6},{... | collective-permute-start | bytes 12296 | tf_op jit(solution)/shard_map/ppermute | solution.py:15
  183.0 3.2 collective-permute-start.23
  183.1 3.2 collective-permute-start.24
  188.3 4.1 %copy-start.45 = (f32[4,4,64,128]{3,1,2,0:T(4,128)}, f32[4,4,64,128]{3,1,2,0:T(4,128)S(1)}, u32[]{:S(2)}) copy-start(f32[4,4,64,128]{3,1,2,0:T(4,128)S(1)} %multiply_add_fusion) | copy-start | bytes 1572868
  188.3 16.0 %collective-permute-start.25 = (f32[4,4,64,128]{3,1,2,0:T(4,128)S(1)}, f32[4,4,64,128]{3,1,2,0:T(4,128)S(1)}, u32[]{:S(2)}, u32[]{:S(2)}) collective-permute-start(f32[4,4,64,128]{3,1,2,0:T(4,128)S(1)} %multiply_add_fusion), channel_id=1, source_target_pairs={{0,16},{1,17},{2,18},{3,19},{4,20},{5,21},{6,22},{7,23},{8,24},{9,... | collective-permute-start | bytes 1572872 | tf_op jit(solution)/shard_map/ppermute | solution.py:23
  192.4 12.7 %copy-start.16 = (f32[1,4,4,64,128]{4,3,2,1,0:T(8,128)S(1)}, f32[1,4,4,64,128]{4,3,2,1,0:T(8,128)}, u32[]{:S(2)}) copy-start(f32[1,4,4,64,128]{4,3,2,1,0:T(8,128)} %param.14) | copy-start | bytes 1572868
  192.4 12.7 %copy-start.18 = (f32[4,4,64,128]{3,1,2,0:T(4,128)S(1)}, f32[4,4,64,128]{3,1,2,0:T(4,128)}, u32[]{:S(2)}) copy-start(f32[4,4,64,128]{3,1,2,0:T(4,128)} %copy-done.17) | copy-start | bytes 1572868
  205.1 3.7 %copy-start.31 = (f32[1,2,64,128]{3,2,1,0:T(8,128)S(1)}, f32[1,2,64,128]{3,2,1,0:T(8,128)}, u32[]{:S(2)}) copy-start(f32[1,2,64,128]{3,2,1,0:T(8,128)} %param.13) | copy-start | bytes 196612
  205.1 3.7 %copy-start.49 = (f32[2,4,4]{2,1,0:T(4,128)S(1)}, f32[2,4,4]{2,1,0:T(4,128)}, u32[]{:S(2)}) copy-start(f32[2,4,4]{2,1,0:T(4,128)} %param.17) | copy-start | bytes 388
  205.1 3.7 %copy-start.50 = (f32[1,2,64,128]{3,2,1,0:T(8,128)S(1)}, f32[1,2,64,128]{3,2,1,0:T(8,128)}, u32[]{:S(2)}) copy-start(f32[1,2,64,128]{3,2,1,0:T(8,128)} %param.19) | copy-start | bytes 196612
  (15 other events, 30.4 us)
Sparse Core Ops, SparseCore 0:
  153.2 21.2 all-gather.4
  208.9 21.9 all-gather.6
where the time goes:
time: 341 us; the launch traced here: 334 us
  blocking collectives  80.8 us (24%)
  waiting for transfers between devices  72.7 us (21%)
  local copies, waits for them, and re-layouts  62.8 us (18%)
  other arithmetic  56.8 us (17%)
  starting transfers between devices  34.8 us (10%)
  between operations  23.1 us (7%)
    psum x1, blocking collectives, per_device(): rest_sq = lax.psum(local_rest, ('win', 'tx', 'ty'))  41.2 us
    psum x1, blocking collectives, per_device(): inner, square = lax.psum((local_inner, local_square), ('win', 'tx', 'ty'))  39.6 us
    slice x9, local copies, waits for them, and re-layouts, padded_2(): last = lax.slice_in_dim(value, length - width, length, axis=dim)  23.1 us
    ppermute x12, waiting for transfers between devices, padded_2(): before = lax.ppermute(last, axis, up)  22.8 us
    ppermute x12, starting transfers between devices, padded_2(): after = lax.ppermute(leading, axis, down)  20.7 us
    ppermute x12, waiting for transfers between devices, padded_2(): after = lax.ppermute(leading, axis, down)  19.7 us
    all_gather x2, waiting for transfers between devices, prefix(): everything = lax.all_gather(value, axis)  16 us
    ppermute x2, waiting for transfers between devices, from_behind(): return lax.ppermute(block, axis, route)  14.2 us
  transfers between devices with their start and end apart: 28, of which 11 were waited for; matrix products, arithmetic and copies ran while one was open for 27% of the time, Pallas kernels for 0%

commit v1 on v0

v1 whole, which is shorter than its diff:
```python
import functools
import jax
import jax.numpy as jnp
from jax import lax
from jax.experimental import pallas as pl
from jax.experimental.pallas import tpu as pltpu
from jax.sharding import PartitionSpec as P

MESH = pl.DeviceIdType.MESH
PAD = 8
EAST, WEST, NORTH, SOUTH = range(4)


def kernel(sizes, dual, obs, inc, traj, mv, ov, diff, wgt,
           o_lam, o_obs, o_inc, o_co,
           fld, grd, back, foll, plin, pls, pxs, gin, gout, oend, sbuf, rbuf, red,
           h_send, h_recv, w_send, w_recv, r_send, r_recv):
    nwin, ntx, nty, steps, nf, nlev, rows, nobs, count = sizes
    groups = rows // 8
    win, tx, ty = lax.axis_index("win"), lax.axis_index("tx"), lax.axis_index("ty")
    has_prev, has_next = win > 0, win < nwin - 1
    right, left = lax.rem(tx + 1, ntx), lax.rem(tx + ntx - 1, ntx)
    lane = lax.broadcasted_iota(jnp.int32, (8, 128), 1)
    axes = (("ty", nty, ty), ("tx", ntx, tx), ("win", nwin, win))

    barrier = pltpu.get_barrier_semaphore()
    for name, n, me in axes:
        for j in range(1, n):
            pl.semaphore_signal(barrier, inc=1, device_id={name: lax.rem(me + j, n)}, device_id_type=MESH)

    @pl.when(ty == 0)
    def _():
        rbuf[:, :, :, SOUTH] = jnp.zeros((2, steps, nlev, 8, 128), jnp.float32)

    @pl.when(ty == nty - 1)
    def _():
        rbuf[:, :, :, NORTH] = jnp.zeros((2, steps, nlev, 8, 128), jnp.float32)

    @pl.when(win == nwin - 1)
    def _():
        foll[...] = jnp.zeros(foll.shape, jnp.float32)
        plin[...] = jnp.zeros(plin.shape, jnp.float32)

    pl.semaphore_wait(barrier, (nty - 1) + (ntx - 1) + (nwin - 1))

    def halo(kind, s, c, side):
        to = ({"tx": left}, {"tx": right}, {"ty": ty - 1}, {"ty": ty + 1})[side]
        return pltpu.make_async_remote_copy(
            src_ref=sbuf.at[kind, s, c, side], dst_ref=rbuf.at[kind, s, c, side],
            send_sem=h_send.at[kind, s, c, side], recv_sem=h_recv.at[kind, s, c, side],
            device_id=to, device_id_type=MESH)

    def sides(kind, s, c, act_send, act_recv):
        for side in range(4):
            copy = halo(kind, s, c, side)
            if side in (EAST, WEST):
                if act_send:
                    act_send(copy)
                if act_recv:
                    act_recv(copy)
                continue
            sends = ty > 0 if side == NORTH else ty < nty - 1
            gets = ty < nty - 1 if side == NORTH else ty > 0
            if act_send:
                pl.when(sends)(lambda copy=copy: act_send(copy))
            if act_recv:
                pl.when(gets)(lambda copy=copy: act_recv(copy))

    def start_halo(kind, s, c):
        sides(kind, s, c, lambda d: d.start(), None)

    def wait_halo(kind, s, c):
        sides(kind, s, c, None, lambda d: d.wait_recv())

    def wcopy(what, c):
        src, dst, to = (
            (dual.at[0, :, c], foll.at[c], win - 1),
            (pls.at[c], plin.at[c], win - 1),
            (gout.at[c], gin.at[c], win + 1),
        )[what]
        return pltpu.make_async_remote_copy(
            src_ref=src, dst_ref=dst, send_sem=w_send.at[what, c], recv_sem=w_recv.at[what, c],
            device_id={"win": to}, device_id_type=MESH)

    @pl.when(has_prev)
    def _():
        for c in range(nlev):
            wcopy(0, c).start()

    def loop(n, body):
        def step(i, carry):
            body(i)
            return carry
        lax.fori_loop(0, n, step, 0)

    def span(g):
        return pl.ds(8 * g, 8)

    def winds(s, c, g):
        a, b = traj[0, s, 0, c, span(g), :], traj[0, s, 1, c, span(g), :]
        pa, pb = jnp.maximum(a, 0.0), jnp.maximum(b, 0.0)
        ma, mb = pa - a, pb - b
        return pa, ma, pb, mb, 1.0 - ((pa + ma) + (pb + mb))

    def into(acc, value, column, k):
        return jnp.where(lane == k, pltpu.roll(value, (k - column) % 128, 1), acc)

    def outof(value, message, column, k):
        shift = 127 if column == 127 else 1
        return jnp.where(lane == column, pltpu.roll(message, (column - k) % 128, 1), pltpu.roll(value, shift, 1))

    zero_tile = jnp.zeros((8, 128), jnp.float32)

    def forward_first(c):
        first, last = zero_tile, zero_tile
        for p in range(nf):
            for g in range(groups):
                value = inc[0, p, c, span(g), :]
                fld[0, c, p, pl.ds(PAD + 8 * g, 8), :] = value
                first = into(first, value, 0, p * groups + g)
                last = into(last, value, 127, p * groups + g)
            sbuf[0, 0, c, NORTH, p, :] = inc[0, p, c, 0, :]
            sbuf[0, 0, c, SOUTH, p, :] = inc[0, p, c, rows - 1, :]
        sbuf[0, 0, c, EAST] = first
        sbuf[0, 0, c, WEST] = last
        start_halo(0, 0, c)

    loop(nlev, forward_first)

    def forward(s, c):
        wait_halo(0, s, c)
        now, later = lax.rem(s, 2), lax.rem(s + 1, 2)
        for p in range(nf):
            fld[now, c, p, PAD - 1, :] = rbuf[0, s, c, SOUTH, p, :]
            fld[now, c, p, PAD + rows, :] = rbuf[0, s, c, NORTH, p, :]
        from_east, from_west = rbuf[0, s, c, EAST], rbuf[0, s, c, WEST]
        first, last = zero_tile, zero_tile
        after = jnp.minimum(s + 1, steps - 1)
        for g in range(groups):
            pa, ma, pb, mb, d = winds(s, c, g)
            for p in range(nf):
                k = diff[p, c]
                x = fld[now, c, p, pl.ds(PAD + 8 * g, 8), :]
                north = fld[now, c, p, pl.ds(PAD + 8 * g + 1, 8), :]
                south = fld[now, c, p, pl.ds(PAD + 8 * g - 1, 8), :]
                place = p * groups + g
                east = outof(x, from_east, 127, place)
                west = outof(x, from_west, 0, place)
                new = (d - 4.0 * k) * x + (pa + k) * west + (ma + k) * east + (pb + k) * south + (mb + k) * north
                fld[later, c, p, pl.ds(PAD + 8 * g, 8), :] = new
                first = into(first, new, 0, place)
                last = into(last, new, 127, place)

        @pl.when(s < steps - 1)
        def _():
            for p in range(nf):
                sbuf[0, after, c, NORTH, p, :] = fld[later, c, p, PAD, :]
                sbuf[0, after, c, SOUTH, p, :] = fld[later, c, p, PAD + rows - 1, :]
            sbuf[0, after, c, EAST] = first
            sbuf[0, after, c, WEST] = last
            start_halo(0, after, c)

    loop(steps, lambda s: loop(nlev, lambda c: forward(s, c)))
    moved = fld.at[steps % 2]

    def products(y, w, k, slot, c, p, g):
        pa, ma, pb, mb, d = w
        g_east, g_west = (pa + k) * y, (ma + k) * y
        here = pl.ds(PAD + 8 * g, 8)
        grd[slot, 0, c, p, here, :] = g_east
        grd[slot, 1, c, p, here, :] = g_west
        grd[slot, 2, c, p, here, :] = (pb + k) * y
        grd[slot, 3, c, p, here, :] = (mb + k) * y
        grd[slot, 4, c, p, here, :] = (d - 4.0 * k) * y
        return g_east, g_west

    def ship(t, slot, c, first, last):
        for p in range(nf):
            sbuf[1, t, c, NORTH, p, :] = grd[slot, 2, c, p, PAD, :]
            sbuf[1, t, c, SOUTH, p, :] = grd[slot, 3, c, p, PAD + rows - 1, :]
        sbuf[1, t, c, EAST] = first
        sbuf[1, t, c, WEST] = last
        start_halo(1, t, c)

    def adjoint_first(c):
        @pl.when(has_next)
        def _():
            wcopy(0, c).wait_recv()

        first, last = zero_tile, zero_tile
        for g in range(groups):
            w = winds(steps - 1, c, g)
            for p in range(nf):
                y = -foll[c, p, span(g), :]
                for o in range(nobs):
                    y = y + wgt[o, p, c] * obs[0, o, span(g), :]
                g_east, g_west = products(y, w, diff[p, c], 0, c, p, g)
                first = into(first, g_east, 0, p * groups + g)
                last = into(last, g_west, 127, p * groups + g)
        ship(0, 0, c, first, last)

    loop(nlev, adjoint_first)

    def gathered(t, slot, c, p, g, from_east, from_west):
        here = pl.ds(PAD + 8 * g, 8)
        place = p * groups + g
        east = outof(grd[slot, 0, c, p, here, :], from_east, 127, place)
        west = outof(grd[slot, 1, c, p, here, :], from_west, 0, place)
        north = grd[slot, 2, c, p, pl.ds(PAD + 8 * g + 1, 8), :]
        south = grd[slot, 3, c, p, pl.ds(PAD + 8 * g - 1, 8), :]
        return grd[slot, 4, c, p, here, :] + ((east + west) + (north + south))

    def receive(t, slot, c):
        wait_halo(1, t, c)
        for p in range(nf):
            grd[slot, 2, c, p, PAD + rows, :] = rbuf[1, t, c, NORTH, p, :]
            grd[slot, 3, c, p, PAD - 1, :] = rbuf[1, t, c, SOUTH, p, :]
        return rbuf[1, t, c, EAST], rbuf[1, t, c, WEST]

    def adjoint(t, c):
        slot, other = lax.rem(t, 2), lax.rem(t + 1, 2)
        from_east, from_west = receive(t, slot, c)
        first, last = zero_tile, zero_tile
        for g in range(groups):
            w = winds(steps - 2 - t, c, g)
            for p in range(nf):
                y = gathered(t, slot, c, p, g, from_east, from_west)
                g_east, g_west = products(y, w, diff[p, c], other, c, p, g)
                first = into(first, g_east, 0, p * groups + g)
                last = into(last, g_west, 127, p * groups + g)
        ship(t + 1, other, c, first, last)

    loop(steps - 1, lambda t: loop(nlev, lambda c: adjoint(t, c)))

    def adjoint_last(c):
        slot = (steps - 1) % 2
        from_east, from_west = receive(steps - 1, slot, c)
        for g in range(groups):
            for p in range(nf):
                back[c, p, span(g), :] = gathered(steps - 1, slot, c, p, g, from_east, from_west)

        @pl.when(win == nwin - 1)
        def _():
            pls[c] = dual[0, :, c] + back[c]
            if nwin > 1:
                wcopy(1, c).start()

    loop(nlev, adjoint_last)

    def fold(x):
        return jnp.sum(x.reshape(-1, 8, 128), axis=0)

    def observe(c, carry):
        return tuple(
            sum((wgt[o, p, c] * moved[c, p, pl.ds(PAD, rows), :] for p in range(nf)), carry[o])
            for o in range(nobs))

    ends = lax.fori_loop(0, nlev, observe, tuple(jnp.zeros((rows, 128), jnp.float32) for _ in range(nobs)))
    wv0, vv0 = zero_tile, zero_tile
    for o in range(nobs):
        v = obs[0, o]
        pm = (ov[0, o] * v + ends[o]) / ov[0, o]
        oend[o] = pm
        wv0 = wv0 + fold(pm * v)
        vv0 = vv0 + fold(v * v)

    def squares(c, acc):
        return acc + fold(dual[0, :, c] * dual[0, :, c]) + fold(inc[0, :, c] * inc[0, :, c])

    vv = lax.fori_loop(0, nlev, squares, vv0)

    def suffix(c, acc):
        @pl.when(has_next)
        def _():
            wcopy(1, c).wait_recv()
            pls[c] = dual[0, :, c] + back[c] + plin[c]

        @pl.when(has_next & has_prev)
        def _():
            wcopy(1, c).start()

        lam = dual[0, :, c]
        new = pls[c]
        base = mv[0, :, c] * (lam - new) + inc[0, :, c]
        pxs[c] = base

        @pl.when((win == 0) & has_next)
        def _():
            gout[c] = base - moved[c, :, pl.ds(PAD, rows), :]
            wcopy(2, c).start()

        return acc + fold(new * lam)

    wv = lax.fori_loop(0, nlev, suffix, wv0)

    def prefix(c, acc):
        @pl.when(has_prev)
        def _():
            wcopy(2, c).wait_recv()
            pxs[c] = pxs[c] + gin[c]

        @pl.when(has_prev & has_next)
        def _():
            gout[c] = pxs[c] - moved[c, :, pl.ds(PAD, rows), :]
            wcopy(2, c).start()

        return acc + fold(pxs[c] * inc[0, :, c])

    wv = lax.fori_loop(0, nlev, prefix, wv)

    def total(x):
        return jnp.broadcast_to(jnp.sum(jnp.sum(x, axis=0, keepdims=True), axis=1, keepdims=True), (1, 128))

    def ratio(a, b):
        return jnp.where(b > 0.0, a / jnp.where(b > 0.0, b, 1.0), 0.0)

    wv, vv = total(wv), total(vv)
    h = ratio(wv, vv)

    def residual(c, acc):
        a = pls[c] - h[None] * dual[0, :, c]
        b = pxs[c] - h[None] * inc[0, :, c]
        return acc + fold(a * a) + fold(b * b)

    uu = zero_tile
    for o in range(nobs):
        r = oend[o] - h * obs[0, o]
        uu = uu + fold(r * r)
    uu = total(lax.fori_loop(0, nlev, residual, uu))

    at = 0
    for index, (name, n, me) in enumerate(axes):
        mine = red.at[at + me]
        red[at + me, 0:1, :] = uu
        red[at + me, 1:2, :] = wv
        red[at + me, 2:3, :] = vv

        def swap(j, name=name, n=n, me=me, at=at):
            return pltpu.make_async_remote_copy(
                src_ref=red.at[at + me], dst_ref=red.at[at + me],
                send_sem=r_send.at[at + j], recv_sem=r_recv.at[at + j],
                device_id={name: lax.rem(me + j, n)}, device_id_type=MESH)

        for j in range(1, n):
            swap(j).start()
        for j in range(1, n):
            swap(j).wait_recv()
        parts = [tuple(red[at + i, q:q + 1, :] for q in range(3)) for i in range(n)]
        wv = functools.reduce(lambda a, b: a + b, [q[1] for q in parts])
        vv = functools.reduce(lambda a, b: a + b, [q[2] for q in parts])
        h = ratio(wv, vv)
        uu = functools.reduce(
            lambda a, b: a + b, [q[0] + (ratio(q[1], q[2]) - h) * (ratio(q[1], q[2]) - h) * q[2] for q in parts])
        for j in range(1, n):
            swap(j).wait_send()
        at += n

    h = wv / vv
    scale = jnp.sqrt(uu / count + 1e-06)
    inv = 1.0 / scale
    o_co[0] = jnp.sum(jnp.where(lane[0:1] == 0, h, 0.0))
    o_co[1] = jnp.sum(jnp.where(lane[0:1] == 0, scale, 0.0))

    def finish(c):
        o_lam[0, :, c] = (pls[c] - h[None] * dual[0, :, c]) * inv[None]
        o_inc[0, :, c] = (pxs[c] - h[None] * inc[0, :, c]) * inv[None]

    loop(nlev, finish)
    for o in range(nobs):
        o_obs[0, o] = (oend[o] - h * obs[0, o]) * inv

    def settle(kind, s, c):
        sides(kind, s, c, lambda d: d.wait_send(), None)

    for kind in range(2):
        loop(steps, lambda s, kind=kind: loop(nlev, lambda c: settle(kind, s, c)))

    def settle_windows(c):
        @pl.when(has_prev)
        def _():
            wcopy(0, c).wait_send()
            wcopy(1, c).wait_send()

        @pl.when(has_next)
        def _():
            wcopy(2, c).wait_send()

    loop(nlev, settle_windows)


def per_device(mesh, dual, obs_dual, increment, trajectory, diffusion, obs_weight, model_var, obs_var):
    nwin, ntx, nty = (mesh.shape[a] for a in ("win", "tx", "ty"))
    _, nf, nlev, rows, cols = dual.shape
    nobs, steps = obs_dual.shape[1], trajectory.shape[1]
    assert cols == 128 and rows % 8 == 0 and nf * rows // 8 <= 128 and nf <= 8
    count = (2 * nf * nlev + nobs) * rows * cols * nwin * ntx * nty
    sizes = (nwin, ntx, nty, steps, nf, nlev, rows, nobs, float(count))
    vmem, smem = pl.BlockSpec(memory_space=pltpu.VMEM), pl.BlockSpec(memory_space=pltpu.SMEM)
    chunks = pltpu.VMEM((nlev, nf, rows, cols), jnp.float32)
    messages = pltpu.VMEM((2, steps, nlev, 4, 8, cols), jnp.float32)
    n_red = nwin + ntx + nty
    return pl.pallas_call(
        functools.partial(kernel, sizes),
        out_shape=(
            jax.ShapeDtypeStruct(dual.shape, jnp.float32),
            jax.ShapeDtypeStruct(obs_dual.shape, jnp.float32),
            jax.ShapeDtypeStruct(increment.shape, jnp.float32),
            jax.ShapeDtypeStruct((2,), jnp.float32),
        ),
        in_specs=[vmem] * 6 + [smem] * 2,
        out_specs=(vmem, vmem, vmem, smem),
        scratch_shapes=[
            pltpu.VMEM((2, nlev, nf, rows + 2 * PAD, cols), jnp.float32),
            pltpu.VMEM((2, 5, nlev, nf, rows + 2 * PAD, cols), jnp.float32),
            chunks, chunks, chunks, chunks, chunks, chunks, chunks,
            pltpu.VMEM((nobs, rows, cols), jnp.float32),
            messages, messages,
            pltpu.VMEM((n_red, 8, cols), jnp.float32),
            pltpu.SemaphoreType.DMA((2, steps, nlev, 4)),
            pltpu.SemaphoreType.DMA((2, steps, nlev, 4)),
            pltpu.SemaphoreType.DMA((3, nlev)),
            pltpu.SemaphoreType.DMA((3, nlev)),
            pltpu.SemaphoreType.DMA((n_red,)),
            pltpu.SemaphoreType.DMA((n_red,)),
        ],
        compiler_params=pltpu.CompilerParams(
            collective_id=0, has_side_effects=True, vmem_limit_bytes=48 * 1024 * 1024),
    )(dual, obs_dual, increment, trajectory, model_var, obs_var, diffusion, obs_weight)


def solution(mesh):
    in_specs = (
        P("win", None, None, "ty", "tx"),
        P("win", None, "ty", "tx"),
        P("win", None, None, "ty", "tx"),
        P("win", None, None, None, "ty", "tx"),
        P(),
        P(),
        P("win", None, None, "ty", "tx"),
        P("win", None, "ty", "tx"),
    )
    out_specs = (
        P("win", None, None, "ty", "tx"),
        P("win", None, "ty", "tx"),
        P("win", None, None, "ty", "tx"),
        P(),
    )
    return jax.shard_map(
        functools.partial(per_device, mesh), mesh=mesh, in_specs=in_specs, out_specs=out_specs, check_vma=False
    )
```

time: 341 us -> 104 us (0.30); the launches traced: 334 us -> 104 us
  Pallas kernels: 0 us -> 93 us
  blocking collectives: 80.8 us -> 0 us
  waiting for transfers between devices: 72.7 us -> 0 us
  other arithmetic: 56.8 us -> 0 us
  local copies, waits for them, and re-layouts: 62.8 us -> 10 us
  starting transfers between devices: 34.8 us -> 0 us
  between operations: 23.1 us -> 0.66 us
    pallas_call x0 -> x1, Pallas kernels: none -> 93 us  [per_device(): pl.pallas_call(functools.partial(kernel, sizes), out_shape=(jax.ShapeDtyp...]
    psum x2 -> x0, blocking collectives: 80.8 us -> none  [the longest x1 41.2 us: per_device(): rest_sq = lax.psum(local_rest, ('win', 'tx', 'ty'))]
    ppermute x26 -> x0, waiting for transfers between devices: 56.7 us -> none  [the longest x12 22.8 us: padded_2(): before = lax.ppermute(last, axis, up)]
    ppermute x26 -> x0, starting transfers between devices: 34.7 us -> none  [the longest x12 20.7 us: padded_2(): after = lax.ppermute(leading, axis, down)]
    slice x12 -> x0, local copies, waits for them, and re-layouts: 31.7 us -> none  [the longest x9 23.1 us: padded_2(): last = lax.slice_in_dim(value, length - width, length, axis=dim)]
    ppermute x6 -> x0, local copies, waits for them, and re-layouts: 16.6 us -> none  [the longest x3 8.36 us: padded_2(): before = lax.ppermute(last, axis, up)]
    all_gather x2 -> x0, waiting for transfers between devices: 16 us -> none  [prefix(): everything = lax.all_gather(value, axis)]
    mul x4 -> x0, other arithmetic: 14.2 us -> none  [the longest x3 14.2 us: trimmed(): north = padded[..., 2:, 1:-1] * keep_north]
  transfers between devices with their start and end apart: 28 -> 0, of which waited for: 11 -> 0; matrix products, arithmetic and copies ran while one was open for 27% -> 0% of each run, Pallas kernels for 0% -> 0%
where the time goes in v1:
time: 104 us
  Pallas kernels  93 us (89%)
  local copies, waits for them, and re-layouts  10 us (10%)
    pallas_call x1, Pallas kernels, per_device(): pl.pallas_call(functools.partial(kernel, sizes), out_shape=(jax.ShapeDtyp...  93 us
    unnamed x20, local copies, waits for them, and re-layouts  10 us

profile of v1, /device:TPU:0, one launch (start us, length us, event | category | flops | bytes accessed | tf_op | source)
XLA Modules:
  0.0 103.7 jit_solution(13270016664511300995)
XLA Ops:
  0.6 0.0 copy-start
  0.6 1.1 %copy-done = f32[1,3,2,4,64,128]{5,4,3,2,1,0:T(8,128)S(1)} copy-done((f32[1,3,2,4,64,128]{5,4,3,2,1,0:T(8,128)S(1)}, f32[1,3,2,4,64,128]{5,4,3,2,1,0:T(8,128)}, u32[]{:S(2)}) %copy-start) | copy-done | bytes 786456
  1.8 0.0 copy-start.1
  1.8 1.0 %copy-done.1 = f32[1,4,4,64,128]{4,3,2,1,0:T(8,128)S(1)} copy-done((f32[1,4,4,64,128]{4,3,2,1,0:T(8,128)S(1)}, f32[1,4,4,64,128]{4,3,2,1,0:T(8,128)}, u32[]{:S(2)}) %copy-start.1) | copy-done | bytes 524312
  2.8 0.0 copy-start.2
  2.8 1.0 %copy-done.2 = f32[1,4,4,64,128]{4,3,2,1,0:T(8,128)S(1)} copy-done((f32[1,4,4,64,128]{4,3,2,1,0:T(8,128)S(1)}, f32[1,4,4,64,128]{4,3,2,1,0:T(8,128)}, u32[]{:S(2)}) %copy-start.2) | copy-done | bytes 524312
  3.9 0.0 copy-start.3
  3.9 1.0 %copy-done.3 = f32[1,4,4,64,128]{4,3,2,1,0:T(8,128)S(1)} copy-done((f32[1,4,4,64,128]{4,3,2,1,0:T(8,128)S(1)}, f32[1,4,4,64,128]{4,3,2,1,0:T(8,128)}, u32[]{:S(2)}) %copy-start.3) | copy-done | bytes 524312
  4.9 0.0 copy-start.4
  4.9 0.8 copy-done.4
  5.7 0.0 copy-start.5
  5.7 0.8 copy-done.5
  6.6 0.0 copy-start.6
  6.6 0.7 copy-done.6
  7.3 0.0 copy-start.7
  7.3 0.7 copy-done.7
  7.9 93.0 %shard_map.111 = (f32[1,4,4,64,128]{4,3,2,1,0:T(8,128)S(1)}, f32[1,2,64,128]{3,2,1,0:T(8,128)S(1)}, f32[1,4,4,64,128]{4,3,2,1,0:T(8,128)S(1)}, f32[2]{0:T(128)S(1)}) custom-call(f32[1,4,4,64,128]{4,3,2,1,0:T(8,128)S(1)} %copy-done.1, f32[1,2,64,128]{3,2,1,0:T(8,128)S(1)} %copy-done.4, f32[1,4,4,64,128]{4,3,2,1,0:T(8,128)S(1)} %copy-done.2, ...), custom_call_target="tpu_custom_call" | custom-call | tf_op jit(solution)/shard_map/pallas_call | solution.py:402
  101.0 0.8 copy.16
  101.8 0.6 copy.17
  102.4 0.8 copy.18
  103.2 0.5 copy.19
Async XLA Ops:
  0.6 1.1 %copy-start = (f32[1,3,2,4,64,128]{5,4,3,2,1,0:T(8,128)S(1)}, f32[1,3,2,4,64,128]{5,4,3,2,1,0:T(8,128)}, u32[]{:S(2)}) copy-start(f32[1,3,2,4,64,128]{5,4,3,2,1,0:T(8,128)} %traj.1) | copy-start | bytes 2359300
  1.8 1.0 %copy-start.1 = (f32[1,4,4,64,128]{4,3,2,1,0:T(8,128)S(1)}, f32[1,4,4,64,128]{4,3,2,1,0:T(8,128)}, u32[]{:S(2)}) copy-start(f32[1,4,4,64,128]{4,3,2,1,0:T(8,128)} %dual.1) | copy-start | bytes 1572868
  2.8 1.0 %copy-start.2 = (f32[1,4,4,64,128]{4,3,2,1,0:T(8,128)S(1)}, f32[1,4,4,64,128]{4,3,2,1,0:T(8,128)}, u32[]{:S(2)}) copy-start(f32[1,4,4,64,128]{4,3,2,1,0:T(8,128)} %inc.1) | copy-start | bytes 1572868
  3.9 1.0 %copy-start.3 = (f32[1,4,4,64,128]{4,3,2,1,0:T(8,128)S(1)}, f32[1,4,4,64,128]{4,3,2,1,0:T(8,128)}, u32[]{:S(2)}) copy-start(f32[1,4,4,64,128]{4,3,2,1,0:T(8,128)} %mv.1) | copy-start | bytes 1572868
  4.9 0.8 copy-start.4
  5.7 0.8 copy-start.5
  6.6 0.7 copy-start.6
  7.3 0.7 copy-start.7

commit v2 on v1

--- a/solution.py
+++ b/solution.py
@@ -11,8 +11,9 @@
 EAST, WEST, NORTH, SOUTH = range(4)
 
 
-def kernel(sizes, dual, obs, inc, traj, mv, ov, diff, wgt,
+def kernel(sizes, h_dual, h_obs, h_inc, h_traj, h_mv, h_ov, h_diff, h_wgt,
            o_lam, o_obs, o_inc, o_co,
+           dual, obs, inc, traj, mv, ov, diff, wgt, i_sem,
            fld, grd, back, foll, plin, pls, pxs, gin, gout, oend, sbuf, rbuf, red,
            h_send, h_recv, w_send, w_recv, r_send, r_recv):
     nwin, ntx, nty, steps, nf, nlev, rows, nobs, count = sizes
@@ -23,19 +24,20 @@
     lane = lax.broadcasted_iota(jnp.int32, (8, 128), 1)
     axes = (("ty", nty, ty), ("tx", ntx, tx), ("win", nwin, win))
 
+    brought = [
+        pltpu.make_async_copy(src, dst, i_sem.at[i])
+        for i, (src, dst) in enumerate((
+            (h_inc, inc), (h_diff, diff), (h_traj, traj), (h_obs, obs),
+            (h_wgt, wgt), (h_dual, dual), (h_mv, mv), (h_ov, ov)))
+    ]
+    for copy in brought:
+        copy.start()
+
     barrier = pltpu.get_barrier_semaphore()
     for name, n, me in axes:
         for j in range(1, n):
             pl.semaphore_signal(barrier, inc=1, device_id={name: lax.rem(me + j, n)}, device_id_type=MESH)
 
-    @pl.when(ty == 0)
-    def _():
-        rbuf[:, :, :, SOUTH] = jnp.zeros((2, steps, nlev, 8, 128), jnp.float32)
-
-    @pl.when(ty == nty - 1)
-    def _():
-        rbuf[:, :, :, NORTH] = jnp.zeros((2, steps, nlev, 8, 128), jnp.float32)
-
     @pl.when(win == nwin - 1)
     def _():
         foll[...] = jnp.zeros(foll.shape, jnp.float32)
@@ -43,38 +45,30 @@
 
     pl.semaphore_wait(barrier, (nty - 1) + (ntx - 1) + (nwin - 1))
 
-    def halo(kind, s, c, side):
-        to = ({"tx": left}, {"tx": right}, {"ty": ty - 1}, {"ty": ty + 1})[side]
-        return pltpu.make_async_remote_copy(
-            src_ref=sbuf.at[kind, s, c, side], dst_ref=rbuf.at[kind, s, c, side],
-            send_sem=h_send.at[kind, s, c, side], recv_sem=h_recv.at[kind, s, c, side],
-            device_id=to, device_id_type=MESH)
-
-    def sides(kind, s, c, act_send, act_recv):
+    north_of, south_of = lax.rem(ty + 1, nty), lax.rem(ty + nty - 1, nty)
+    to = ({"tx": left}, {"tx": right}, {"ty": south_of}, {"ty": north_of})
+
+    def start_halo(kind, s, c):
         for side in range(4):
-            copy = halo(kind, s, c, side)
-            if side in (EAST, WEST):
-                if act_send:
-                    act_send(copy)
-                if act_recv:
-                    act_recv(copy)
-                continue
-            sends = ty > 0 if side == NORTH else ty < nty - 1
-            gets = ty < nty - 1 if side == NORTH else ty > 0
-            if act_send:
-                pl.when(sends)(lambda copy=copy: act_send(copy))
-            if act_recv:
-                pl.when(gets)(lambda copy=copy: act_recv(copy))
-
-    def start_halo(kind, s, c):
-        sides(kind, s, c, lambda d: d.start(), None)
+            pltpu.make_async_remote_copy(
+                src_ref=sbuf.at[kind, s, c, side], dst_ref=rbuf.at[kind, s, c, side],
+                send_sem=h_send.at[kind], recv_sem=h_recv.at[kind, s, c],
+                device_id=to[side], device_id_type=MESH).start()
 
     def wait_halo(kind, s, c):
-        sides(kind, s, c, None, lambda d: d.wait_recv())
+        pltpu.make_async_remote_copy(
+            src_ref=sbuf.at[kind, s, c], dst_ref=rbuf.at[kind, s, c],
+            send_sem=h_send.at[kind], recv_sem=h_recv.at[kind, s, c],
+            device_id=to[0], device_id_type=MESH).wait_recv()
+
+    def edge_rows(kind, s, c):
+        north = jnp.where(ty == nty - 1, 0.0, rbuf[kind, s, c, NORTH])
+        south = jnp.where(ty == 0, 0.0, rbuf[kind, s, c, SOUTH])
+        return north, south
 
     def wcopy(what, c):
         src, dst, to = (
-            (dual.at[0, :, c], foll.at[c], win - 1),
+            (h_dual.at[0, :, c], foll.at[c], win - 1),
             (pls.at[c], plin.at[c], win - 1),
             (gout.at[c], gin.at[c], win + 1),
         )[what]
@@ -125,17 +119,22 @@
         sbuf[0, 0, c, WEST] = last
         start_halo(0, 0, c)
 
+    brought[0].wait()
     loop(nlev, forward_first)
+    brought[1].wait()
+    brought[2].wait()
 
     def forward(s, c):
         wait_halo(0, s, c)
         now, later = lax.rem(s, 2), lax.rem(s + 1, 2)
+        north_row, south_row = edge_rows(0, s, c)
         for p in range(nf):
-            fld[now, c, p, PAD - 1, :] = rbuf[0, s, c, SOUTH, p, :]
-            fld[now, c, p, PAD + rows, :] = rbuf[0, s, c, NORTH, p, :]
+            fld[now, c, p, PAD - 1, :] = south_row[p]
+            fld[now, c, p, PAD + rows, :] = north_row[p]
         from_east, from_west = rbuf[0, s, c, EAST], rbuf[0, s, c, WEST]
         first, last = zero_tile, zero_tile
         after = jnp.minimum(s + 1, steps - 1)
+        fresh = []
         for g in range(groups):
             pa, ma, pb, mb, d = winds(s, c, g)
             for p in range(nf):
@@ -147,9 +146,11 @@
                 east = outof(x, from_east, 127, place)
                 west = outof(x, from_west, 0, place)
                 new = (d - 4.0 * k) * x + (pa + k) * west + (ma + k) * east + (pb + k) * south + (mb + k) * north
-                fld[later, c, p, pl.ds(PAD + 8 * g, 8), :] = new
+                fresh.append((p, g, new))
                 first = into(first, new, 0, place)
                 last = into(last, new, 127, place)
+        for p, g, new in fresh:
+            fld[later, c, p, pl.ds(PAD + 8 * g, 8), :] = new
 
         @pl.when(s < steps - 1)
         def _():
@@ -182,19 +183,26 @@
         sbuf[1, t, c, WEST] = last
         start_halo(1, t, c)
 
+    brought[3].wait()
+    brought[4].wait()
+
     def adjoint_first(c):
         @pl.when(has_next)
         def _():
             wcopy(0, c).wait_recv()
 
         first, last = zero_tile, zero_tile
+        start = {}
         for g in range(groups):
-            w = winds(steps - 1, c, g)
             for p in range(nf):
                 y = -foll[c, p, span(g), :]
                 for o in range(nobs):
                     y = y + wgt[o, p, c] * obs[0, o, span(g), :]
-                g_east, g_west = products(y, w, diff[p, c], 0, c, p, g)
+                start[p, g] = y
+        for g in range(groups):
+            w = winds(steps - 1, c, g)
+            for p in range(nf):
+                g_east, g_west = products(start[p, g], w, diff[p, c], 0, c, p, g)
                 first = into(first, g_east, 0, p * groups + g)
                 last = into(last, g_west, 127, p * groups + g)
         ship(0, 0, c, first, last)
@@ -212,20 +220,23 @@
 
     def receive(t, slot, c):
         wait_halo(1, t, c)
+        north_row, south_row = edge_rows(1, t, c)
         for p in range(nf):
-            grd[slot, 2, c, p, PAD + rows, :] = rbuf[1, t, c, NORTH, p, :]
-            grd[slot, 3, c, p, PAD - 1, :] = rbuf[1, t, c, SOUTH, p, :]
+            grd[slot, 2, c, p, PAD + rows, :] = north_row[p]
+            grd[slot, 3, c, p, PAD - 1, :] = south_row[p]
         return rbuf[1, t, c, EAST], rbuf[1, t, c, WEST]
 
     def adjoint(t, c):
         slot, other = lax.rem(t, 2), lax.rem(t + 1, 2)
         from_east, from_west = receive(t, slot, c)
         first, last = zero_tile, zero_tile
+        start = {
+            (p, g): gathered(t, slot, c, p, g, from_east, from_west)
+            for g in range(groups) for p in range(nf)}
         for g in range(groups):
             w = winds(steps - 2 - t, c, g)
             for p in range(nf):
-                y = gathered(t, slot, c, p, g, from_east, from_west)
-                g_east, g_west = products(y, w, diff[p, c], other, c, p, g)
+                g_east, g_west = products(start[p, g], w, diff[p, c], other, c, p, g)
                 first = into(first, g_east, 0, p * groups + g)
                 last = into(last, g_west, 127, p * groups + g)
         ship(t + 1, other, c, first, last)
@@ -235,9 +246,11 @@
     def adjoint_last(c):
         slot = (steps - 1) % 2
         from_east, from_west = receive(steps - 1, slot, c)
-        for g in range(groups):
-            for p in range(nf):
-                back[c, p, span(g), :] = gathered(steps - 1, slot, c, p, g, from_east, from_west)
+        done = {
+            (p, g): gathered(steps - 1, slot, c, p, g, from_east, from_west)
+            for g in range(groups) for p in range(nf)}
+        for (p, g), y in done.items():
+            back[c, p, span(g), :] = y
 
         @pl.when(win == nwin - 1)
         def _():
@@ -245,7 +258,10 @@
             if nwin > 1:
                 wcopy(1, c).start()
 
+    brought[5].wait()
     loop(nlev, adjoint_last)
+    brought[6].wait()
+    brought[7].wait()
 
     def fold(x):
         return jnp.sum(x.reshape(-1, 8, 128), axis=0)
@@ -369,13 +385,12 @@
     for o in range(nobs):
         o_obs[0, o] = (oend[o] - h * obs[0, o]) * inv
 
-    def settle(kind, s, c):
-        sides(kind, s, c, lambda d: d.wait_send(), None)
-
     for kind in range(2):
-        loop(steps, lambda s, kind=kind: loop(nlev, lambda c: settle(kind, s, c)))
-
-    def settle_windows(c):
+        pltpu.make_async_remote_copy(
+            src_ref=sbuf.at[kind], dst_ref=rbuf.at[kind], send_sem=h_send.at[kind],
+            recv_sem=h_recv.at[kind, 0, 0], device_id=to[0], device_id_type=MESH).wait_send()
+
+    def settle(c):
         @pl.when(has_prev)
         def _():
             wcopy(0, c).wait_send()
@@ -385,7 +400,7 @@
         def _():
             wcopy(2, c).wait_send()
 
-    loop(nlev, settle_windows)
+    loop(nlev, settle)
 
 
 def per_device(mesh, dual, obs_dual, increment, trajectory, diffusion, obs_weight, model_var, obs_var):
@@ -407,17 +422,22 @@
             jax.ShapeDtypeStruct(increment.shape, jnp.float32),
             jax.ShapeDtypeStruct((2,), jnp.float32),
         ),
-        in_specs=[vmem] * 6 + [smem] * 2,
+        in_specs=[pl.BlockSpec(memory_space=pltpu.HBM)] * 8,
         out_specs=(vmem, vmem, vmem, smem),
         scratch_shapes=[
+            pltpu.VMEM(dual.shape, jnp.float32), pltpu.VMEM(obs_dual.shape, jnp.float32),
+            pltpu.VMEM(increment.shape, jnp.float32), pltpu.VMEM(trajectory.shape, jnp.float32),
+            pltpu.VMEM(model_var.shape, jnp.float32), pltpu.VMEM(obs_var.shape, jnp.float32),
+            pltpu.SMEM(diffusion.shape, jnp.float32), pltpu.SMEM(obs_weight.shape, jnp.float32),
+            pltpu.SemaphoreType.DMA((8,)),
             pltpu.VMEM((2, nlev, nf, rows + 2 * PAD, cols), jnp.float32),
             pltpu.VMEM((2, 5, nlev, nf, rows + 2 * PAD, cols), jnp.float32),
             chunks, chunks, chunks, chunks, chunks, chunks, chunks,
             pltpu.VMEM((nobs, rows, cols), jnp.float32),
             messages, messages,
             pltpu.VMEM((n_red, 8, cols), jnp.float32),
-            pltpu.SemaphoreType.DMA((2, steps, nlev, 4)),
-            pltpu.SemaphoreType.DMA((2, steps, nlev, 4)),
+            pltpu.SemaphoreType.DMA((2,)),
+            pltpu.SemaphoreType.DMA((2, steps, nlev)),
             pltpu.SemaphoreType.DMA((3, nlev)),
             pltpu.SemaphoreType.DMA((3, nlev)),
             pltpu.SemaphoreType.DMA((n_red,)),

time: 104 us -> 72 us (0.69)
  Pallas kernels: 93 us -> 60.9 us
    pallas_call x1, Pallas kernels: 93 us -> 60.9 us  [per_device(): pl.pallas_call(functools.partial(kernel, sizes), out_shape=(jax.ShapeDtyp...]
where the time goes in v2:
time: 72 us; the launch traced here: 71.5 us
  Pallas kernels  60.9 us (85%)
  local copies, waits for them, and re-layouts  10 us (14%)
    pallas_call x1, Pallas kernels, per_device(): pl.pallas_call(functools.partial(kernel, sizes), out_shape=(jax.ShapeDtyp...  60.9 us
    unnamed x20, local copies, waits for them, and re-layouts  10 us

profile of v2, /device:TPU:0, one launch (start us, length us, event | category | flops | bytes accessed | tf_op | source)
XLA Modules:
  0.0 71.5 jit_solution(4689559661444648563)
XLA Ops:
  0.6 0.0 copy-start
  0.6 1.1 %copy-done = f32[1,3,2,4,64,128]{5,4,3,2,1,0:T(8,128)S(1)} copy-done((f32[1,3,2,4,64,128]{5,4,3,2,1,0:T(8,128)S(1)}, f32[1,3,2,4,64,128]{5,4,3,2,1,0:T(8,128)}, u32[]{:S(2)}) %copy-start) | copy-done | bytes 786456
  1.8 0.0 copy-start.1
  1.8 1.0 %copy-done.1 = f32[1,4,4,64,128]{4,3,2,1,0:T(8,128)S(1)} copy-done((f32[1,4,4,64,128]{4,3,2,1,0:T(8,128)S(1)}, f32[1,4,4,64,128]{4,3,2,1,0:T(8,128)}, u32[]{:S(2)}) %copy-start.1) | copy-done | bytes 524312
  2.8 0.0 copy-start.2
  2.8 1.0 %copy-done.2 = f32[1,4,4,64,128]{4,3,2,1,0:T(8,128)S(1)} copy-done((f32[1,4,4,64,128]{4,3,2,1,0:T(8,128)S(1)}, f32[1,4,4,64,128]{4,3,2,1,0:T(8,128)}, u32[]{:S(2)}) %copy-start.2) | copy-done | bytes 524312
  3.9 0.0 copy-start.3
  3.9 1.0 %copy-done.3 = f32[1,4,4,64,128]{4,3,2,1,0:T(8,128)S(1)} copy-done((f32[1,4,4,64,128]{4,3,2,1,0:T(8,128)S(1)}, f32[1,4,4,64,128]{4,3,2,1,0:T(8,128)}, u32[]{:S(2)}) %copy-start.3) | copy-done | bytes 524312
  4.9 0.0 copy-start.4
  4.9 0.8 %copy-done.4 = f32[1,2,64,128]{3,2,1,0:T(8,128)S(1)} copy-done((f32[1,2,64,128]{3,2,1,0:T(8,128)S(1)}, f32[1,2,64,128]{3,2,1,0:T(8,128)}, u32[]{:S(2)}) %copy-start.4) | copy-done | bytes 65560
  5.7 0.0 copy-start.5
  5.7 0.8 %copy-done.5 = f32[1,2,64,128]{3,2,1,0:T(8,128)S(1)} copy-done((f32[1,2,64,128]{3,2,1,0:T(8,128)S(1)}, f32[1,2,64,128]{3,2,1,0:T(8,128)}, u32[]{:S(2)}) %copy-start.5) | copy-done | bytes 65560
  6.6 0.0 copy-start.6
  6.6 0.7 copy-done.6
  7.3 0.0 copy-start.7
  7.3 0.7 copy-done.7
  7.9 60.9 %shard_map.111 = (f32[1,4,4,64,128]{4,3,2,1,0:T(8,128)S(1)}, f32[1,2,64,128]{3,2,1,0:T(8,128)S(1)}, f32[1,4,4,64,128]{4,3,2,1,0:T(8,128)S(1)}, f32[2]{0:T(128)S(1)}) custom-call(f32[1,4,4,64,128]{4,3,2,1,0:T(8,128)S(1)} %copy-done.1, f32[1,2,64,128]{3,2,1,0:T(8,128)S(1)} %copy-done.4, f32[1,4,4,64,128]{4,3,2,1,0:T(8,128)S(1)} %copy-done.2, ...), custom_call_target="tpu_custom_call" | custom-call | tf_op jit(solution)/shard_map/pallas_call | solution.py:417
  68.8 0.8 %copy.16 = f32[1,4,4,64,128]{4,3,2,1,0:T(8,128)} copy(f32[1,4,4,64,128]{4,3,2,1,0:T(8,128)S(1)} %get-tuple-element.8) | data formatting | bytes 1048576
  69.6 0.6 copy.17
  70.2 0.8 %copy.18 = f32[1,4,4,64,128]{4,3,2,1,0:T(8,128)} copy(f32[1,4,4,64,128]{4,3,2,1,0:T(8,128)S(1)} %get-tuple-element.10) | data formatting | bytes 1048576
  71.0 0.5 copy.19
Async XLA Ops:
  0.6 1.1 %copy-start = (f32[1,3,2,4,64,128]{5,4,3,2,1,0:T(8,128)S(1)}, f32[1,3,2,4,64,128]{5,4,3,2,1,0:T(8,128)}, u32[]{:S(2)}) copy-start(f32[1,3,2,4,64,128]{5,4,3,2,1,0:T(8,128)} %h_traj.1) | copy-start | bytes 2359300
  1.8 1.0 %copy-start.1 = (f32[1,4,4,64,128]{4,3,2,1,0:T(8,128)S(1)}, f32[1,4,4,64,128]{4,3,2,1,0:T(8,128)}, u32[]{:S(2)}) copy-start(f32[1,4,4,64,128]{4,3,2,1,0:T(8,128)} %h_dual.1) | copy-start | bytes 1572868
  2.8 1.0 %copy-start.2 = (f32[1,4,4,64,128]{4,3,2,1,0:T(8,128)S(1)}, f32[1,4,4,64,128]{4,3,2,1,0:T(8,128)}, u32[]{:S(2)}) copy-start(f32[1,4,4,64,128]{4,3,2,1,0:T(8,128)} %h_inc.1) | copy-start | bytes 1572868
  3.9 1.0 %copy-start.3 = (f32[1,4,4,64,128]{4,3,2,1,0:T(8,128)S(1)}, f32[1,4,4,64,128]{4,3,2,1,0:T(8,128)}, u32[]{:S(2)}) copy-start(f32[1,4,4,64,128]{4,3,2,1,0:T(8,128)} %h_mv.1) | copy-start | bytes 1572868
  4.9 0.8 %copy-start.4 = (f32[1,2,64,128]{3,2,1,0:T(8,128)S(1)}, f32[1,2,64,128]{3,2,1,0:T(8,128)}, u32[]{:S(2)}) copy-start(f32[1,2,64,128]{3,2,1,0:T(8,128)} %h_obs.1) | copy-start | bytes 196612
  5.7 0.8 %copy-start.5 = (f32[1,2,64,128]{3,2,1,0:T(8,128)S(1)}, f32[1,2,64,128]{3,2,1,0:T(8,128)}, u32[]{:S(2)}) copy-start(f32[1,2,64,128]{3,2,1,0:T(8,128)} %h_ov.1) | copy-start | bytes 196612
  6.6 0.7 copy-start.6
  7.3 0.7 copy-start.7

commit v3 on v2

--- a/solution.py
+++ b/solution.py
@@ -96,33 +96,36 @@
         ma, mb = pa - a, pb - b
         return pa, ma, pb, mb, 1.0 - ((pa + ma) + (pb + mb))
 
-    def into(acc, value, column, k):
-        return jnp.where(lane == k, pltpu.roll(value, (k - column) % 128, 1), acc)
-
-    def outof(value, message, column, k):
-        shift = 127 if column == 127 else 1
-        return jnp.where(lane == column, pltpu.roll(message, (column - k) % 128, 1), pltpu.roll(value, shift, 1))
+    pair = lane >> 1
+
+    def into(acc, value, k):
+        return jnp.where(pair == k, pltpu.roll(value, 2 * k + 1, 1), acc)
+
+    def edge_columns(kind, s, c):
+        return jnp.where(
+            lane == 2 * pair, pltpu.roll(rbuf[kind, s, c, EAST], 127, 1), pltpu.roll(rbuf[kind, s, c, WEST], 1, 1))
+
+    def shifted(for_east, for_west, columns, k):
+        edge = pltpu.roll(columns, (127 - 2 * k) % 128, 1)
+        east = jnp.where(lane == 127, edge, pltpu.roll(for_east, 127, 1))
+        west = jnp.where(lane == 0, edge, pltpu.roll(for_west, 1, 1))
+        return east, west
 
     zero_tile = jnp.zeros((8, 128), jnp.float32)
 
     def forward_first(c):
-        first, last = zero_tile, zero_tile
+        packed = zero_tile
         for p in range(nf):
             for g in range(groups):
                 value = inc[0, p, c, span(g), :]
                 fld[0, c, p, pl.ds(PAD + 8 * g, 8), :] = value
-                first = into(first, value, 0, p * groups + g)
-                last = into(last, value, 127, p * groups + g)
+                packed = into(packed, value, p * groups + g)
             sbuf[0, 0, c, NORTH, p, :] = inc[0, p, c, 0, :]
             sbuf[0, 0, c, SOUTH, p, :] = inc[0, p, c, rows - 1, :]
-        sbuf[0, 0, c, EAST] = first
-        sbuf[0, 0, c, WEST] = last
+        sbuf[0, 0, c, EAST] = packed
+        sbuf[0, 0, c, WEST] = packed
         start_halo(0, 0, c)
 
-    brought[0].wait()
-    loop(nlev, forward_first)
-    brought[1].wait()
-    brought[2].wait()
 
     def forward(s, c):
         wait_halo(0, s, c)
@@ -131,24 +134,23 @@
         for p in range(nf):
             fld[now, c, p, PAD - 1, :] = south_row[p]
             fld[now, c, p, PAD + rows, :] = north_row[p]
-        from_east, from_west = rbuf[0, s, c, EAST], rbuf[0, s, c, WEST]
-        first, last = zero_tile, zero_tile
+        columns = edge_columns(0, s, c)
+        packed = zero_tile
+        ks = [diff[p, c] for p in range(nf)]
         after = jnp.minimum(s + 1, steps - 1)
         fresh = []
         for g in range(groups):
             pa, ma, pb, mb, d = winds(s, c, g)
             for p in range(nf):
-                k = diff[p, c]
+                k = ks[p]
                 x = fld[now, c, p, pl.ds(PAD + 8 * g, 8), :]
                 north = fld[now, c, p, pl.ds(PAD + 8 * g + 1, 8), :]
                 south = fld[now, c, p, pl.ds(PAD + 8 * g - 1, 8), :]
                 place = p * groups + g
-                east = outof(x, from_east, 127, place)
-                west = outof(x, from_west, 0, place)
+                east, west = shifted(x, x, columns, place)
                 new = (d - 4.0 * k) * x + (pa + k) * west + (ma + k) * east + (pb + k) * south + (mb + k) * north
                 fresh.append((p, g, new))
-                first = into(first, new, 0, place)
-                last = into(last, new, 127, place)
+                packed = into(packed, new, place)
         for p, g, new in fresh:
             fld[later, c, p, pl.ds(PAD + 8 * g, 8), :] = new
 
@@ -157,11 +159,10 @@
             for p in range(nf):
                 sbuf[0, after, c, NORTH, p, :] = fld[later, c, p, PAD, :]
                 sbuf[0, after, c, SOUTH, p, :] = fld[later, c, p, PAD + rows - 1, :]
-            sbuf[0, after, c, EAST] = first
-            sbuf[0, after, c, WEST] = last
+            sbuf[0, after, c, EAST] = packed
+            sbuf[0, after, c, WEST] = packed
             start_halo(0, after, c)
 
-    loop(steps, lambda s: loop(nlev, lambda c: forward(s, c)))
     moved = fld.at[steps % 2]
 
     def products(y, w, k, slot, c, p, g):
@@ -173,47 +174,42 @@
         grd[slot, 2, c, p, here, :] = (pb + k) * y
         grd[slot, 3, c, p, here, :] = (mb + k) * y
         grd[slot, 4, c, p, here, :] = (d - 4.0 * k) * y
-        return g_east, g_west
-
-    def ship(t, slot, c, first, last):
+        return jnp.where(lane == 0, g_east, g_west)
+
+    def ship(t, slot, c, packed):
         for p in range(nf):
             sbuf[1, t, c, NORTH, p, :] = grd[slot, 2, c, p, PAD, :]
             sbuf[1, t, c, SOUTH, p, :] = grd[slot, 3, c, p, PAD + rows - 1, :]
-        sbuf[1, t, c, EAST] = first
-        sbuf[1, t, c, WEST] = last
+        sbuf[1, t, c, EAST] = packed
+        sbuf[1, t, c, WEST] = packed
         start_halo(1, t, c)
-
-    brought[3].wait()
-    brought[4].wait()
 
     def adjoint_first(c):
         @pl.when(has_next)
         def _():
             wcopy(0, c).wait_recv()
 
-        first, last = zero_tile, zero_tile
+        packed = zero_tile
+        ks = [diff[p, c] for p in range(nf)]
+        ws = [[wgt[o, p, c] for o in range(nobs)] for p in range(nf)]
         start = {}
         for g in range(groups):
+            observed = [obs[0, o, span(g), :] for o in range(nobs)]
             for p in range(nf):
                 y = -foll[c, p, span(g), :]
                 for o in range(nobs):
-                    y = y + wgt[o, p, c] * obs[0, o, span(g), :]
+                    y = y + ws[p][o] * observed[o]
                 start[p, g] = y
         for g in range(groups):
             w = winds(steps - 1, c, g)
             for p in range(nf):
-                g_east, g_west = products(start[p, g], w, diff[p, c], 0, c, p, g)
-                first = into(first, g_east, 0, p * groups + g)
-                last = into(last, g_west, 127, p * groups + g)
-        ship(0, 0, c, first, last)
-
-    loop(nlev, adjoint_first)
-
-    def gathered(t, slot, c, p, g, from_east, from_west):
+                packed = into(packed, products(start[p, g], w, ks[p], 0, c, p, g), p * groups + g)
+        ship(0, 0, c, packed)
+
+
+    def gathered(slot, c, p, g, columns):
         here = pl.ds(PAD + 8 * g, 8)
-        place = p * groups + g
-        east = outof(grd[slot, 0, c, p, here, :], from_east, 127, place)
-        west = outof(grd[slot, 1, c, p, here, :], from_west, 0, place)
+        east, west = shifted(grd[slot, 0, c, p, here, :], grd[slot, 1, c, p, here, :], columns, p * groups + g)
         north = grd[slot, 2, c, p, pl.ds(PAD + 8 * g + 1, 8), :]
         south = grd[slot, 3, c, p, pl.ds(PAD + 8 * g - 1, 8), :]
         return grd[slot, 4, c, p, here, :] + ((east + west) + (north + south))
@@ -224,30 +220,28 @@
         for p in range(nf):
             grd[slot, 2, c, p, PAD + rows, :] = north_row[p]
             grd[slot, 3, c, p, PAD - 1, :] = south_row[p]
-        return rbuf[1, t, c, EAST], rbuf[1, t, c, WEST]
+        return edge_columns(1, t, c)
 
     def adjoint(t, c):
         slot, other = lax.rem(t, 2), lax.rem(t + 1, 2)
-        from_east, from_west = receive(t, slot, c)
-        first, last = zero_tile, zero_tile
+        columns = receive(t, slot, c)
+        packed = zero_tile
+        ks = [diff[p, c] for p in range(nf)]
         start = {
-            (p, g): gathered(t, slot, c, p, g, from_east, from_west)
+            (p, g): gathered(slot, c, p, g, columns)
             for g in range(groups) for p in range(nf)}
         for g in range(groups):
             w = winds(steps - 2 - t, c, g)
             for p in range(nf):
-                g_east, g_west = products(start[p, g], w, diff[p, c], other, c, p, g)
-                first = into(first, g_east, 0, p * groups + g)
-                last = into(last, g_west, 127, p * groups + g)
-        ship(t + 1, other, c, first, last)
-
-    loop(steps - 1, lambda t: loop(nlev, lambda c: adjoint(t, c)))
+                packed = into(packed, products(start[p, g], w, ks[p], other, c, p, g), p * groups + g)
+        ship(t + 1, other, c, packed)
+
 
     def adjoint_last(c):
         slot = (steps - 1) % 2
-        from_east, from_west = receive(steps - 1, slot, c)
+        columns = receive(steps - 1, slot, c)
         done = {
-            (p, g): gathered(steps - 1, slot, c, p, g, from_east, from_west)
+            (p, g): gathered(slot, c, p, g, columns)
             for g in range(groups) for p in range(nf)}
         for (p, g), y in done.items():
             back[c, p, span(g), :] = y
@@ -258,10 +252,24 @@
             if nwin > 1:
                 wcopy(1, c).start()
 
-    brought[5].wait()
-    loop(nlev, adjoint_last)
-    brought[6].wait()
-    brought[7].wait()
+    for copy in brought:
+        copy.wait()
+
+    def model(stage):
+        now = lax.rem(stage + jnp.where(win == nwin - 1, 1, 0), 2)
+
+        @pl.when(now == 0)
+        def _():
+            loop(nlev, forward_first)
+            loop(steps, lambda s: loop(nlev, lambda c: forward(s, c)))
+
+        @pl.when(now == 1)
+        def _():
+            loop(nlev, adjoint_first)
+            loop(steps - 1, lambda t: loop(nlev, lambda c: adjoint(t, c)))
+            loop(nlev, adjoint_last)
+
+    loop(2, model)
 
     def fold(x):
         return jnp.sum(x.reshape(-1, 8, 128), axis=0)
@@ -407,7 +415,7 @@
     nwin, ntx, nty = (mesh.shape[a] for a in ("win", "tx", "ty"))
     _, nf, nlev, rows, cols = dual.shape
     nobs, steps = obs_dual.shape[1], trajectory.shape[1]
-    assert cols == 128 and rows % 8 == 0 and nf * rows // 8 <= 128 and nf <= 8
+    assert cols == 128 and rows % 8 == 0 and nf * rows // 4 <= 128 and nf <= 8
     count = (2 * nf * nlev + nobs) * rows * cols * nwin * ntx * nty
     sizes = (nwin, ntx, nty, steps, nf, nlev, rows, nobs, float(count))
     vmem, smem = pl.BlockSpec(memory_space=pltpu.VMEM), pl.BlockSpec(memory_space=pltpu.SMEM)
@@ -444,7 +452,7 @@
             pltpu.SemaphoreType.DMA((n_red,)),
         ],
         compiler_params=pltpu.CompilerParams(
-            collective_id=0, has_side_effects=True, vmem_limit_bytes=48 * 1024 * 1024),
+            collective_id=0, has_side_effects=True, vmem_limit_bytes=60 * 1024 * 1024),
     )(dual, obs_dual, increment, trajectory, model_var, obs_var, diffusion, obs_weight)
 
 

time: 72 us -> 58.9 us (0.82)
  Pallas kernels: 60.9 us -> 54.2 us
  local copies, waits for them, and re-layouts: 10 us -> 3.89 us
    pallas_call x1, Pallas kernels: 60.9 us -> 54.2 us  [per_device(): pl.pallas_call(functools.partial(kernel, sizes), out_shape=(jax.ShapeDtyp...]
    unnamed x20 -> x10, local copies, waits for them, and re-layouts: 10 us -> 3.89 us
where the time goes in v3:
time: 58.9 us; the launch traced here: 58.8 us
  Pallas kernels  54.2 us (92%)
  local copies, waits for them, and re-layouts  3.89 us (7%)
  between operations  0.66 us (1%)
    pallas_call x1, Pallas kernels, per_device(): pl.pallas_call(functools.partial(kernel, sizes), out_shape=(jax.ShapeDtyp...  54.2 us
    unnamed x10, local copies, waits for them, and re-layouts  3.89 us

profile of v3, /device:TPU:0, one launch (start us, length us, event | category | flops | bytes accessed | tf_op | source)
XLA Modules:
  0.0 58.8 jit_solution(3714185926188613383)
XLA Ops:
  0.6 54.2 %shard_map.111 = (f32[1,4,4,64,128]{4,3,2,1,0:T(8,128)}, f32[1,2,64,128]{3,2,1,0:T(8,128)}, f32[1,4,4,64,128]{4,3,2,1,0:T(8,128)}, f32[2]{0:T(128)}) custom-call(f32[1,4,4,64,128]{4,3,2,1,0:T(8,128)} %h_dual.1, f32[1,2,64,128]{3,2,1,0:T(8,128)} %h_obs.1, f32[1,4,4,64,128]{4,3,2,1,0:T(8,128)} %h_inc.1, f32[1,3,2,4,64,128]{5,4,3,2,1,0:T(8,128)} %h_traj.1, ...), custom_call_target="tpu_custom_call" | custom-call | tf_op jit(solution)/shard_map/pallas_call | solution.py:425
  54.9 0.0 copy-start.1
  54.9 0.0 copy-start
  54.9 1.9 %copy.16 = f32[1,4,4,64,128]{4,3,2,1,0:T(8,128)} copy(f32[1,4,4,64,128]{4,3,2,1,0:T(8,128)} %get-tuple-element.8) | data formatting | bytes 1048576
  56.8 0.0 copy-done.1
  56.8 0.6 %copy.17 = f32[1,2,64,128]{3,2,1,0:T(8,128)} copy(f32[1,2,64,128]{3,2,1,0:T(8,128)S(1)} %copy-done.1) | data formatting | bytes 131072
  57.5 0.0 copy-done
  57.5 0.0 copy-start.2
  57.5 0.8 %copy.18 = f32[1,4,4,64,128]{4,3,2,1,0:T(8,128)} copy(f32[1,4,4,64,128]{4,3,2,1,0:T(8,128)S(1)} %copy-done) | data formatting | bytes 1048576
  58.3 0.0 copy-done.2
  58.3 0.5 copy.19
Async XLA Ops:
  54.9 2.0 %copy-start.1 = (f32[1,2,64,128]{3,2,1,0:T(8,128)S(1)}, f32[1,2,64,128]{3,2,1,0:T(8,128)}, u32[]{:S(2)}) copy-start(f32[1,2,64,128]{3,2,1,0:T(8,128)} %get-tuple-element.9) | copy-start | bytes 196612
  54.9 2.6 %copy-start = (f32[1,4,4,64,128]{4,3,2,1,0:T(8,128)S(1)}, f32[1,4,4,64,128]{4,3,2,1,0:T(8,128)}, u32[]{:S(2)}) copy-start(f32[1,4,4,64,128]{4,3,2,1,0:T(8,128)} %get-tuple-element.10) | copy-start | bytes 1572868
  57.5 0.8 %copy-start.2 = (f32[2]{0:T(128)S(1)}, f32[2]{0:T(128)}, u32[]{:S(2)}) copy-start(f32[2]{0:T(128)} %get-tuple-element.11) | copy-start | bytes 28

commit v4 on v3

--- a/solution.py
+++ b/solution.py
@@ -15,14 +15,20 @@
            o_lam, o_obs, o_inc, o_co,
            dual, obs, inc, traj, mv, ov, diff, wgt, i_sem,
            fld, grd, back, foll, plin, pls, pxs, gin, gout, oend, sbuf, rbuf, red,
-           h_send, h_recv, w_send, w_recv, r_send, r_recv):
+           wsum, h_send, h_recv, w_send, w_recv, r_send, r_recv):
     nwin, ntx, nty, steps, nf, nlev, rows, nobs, count = sizes
     groups = rows // 8
     win, tx, ty = lax.axis_index("win"), lax.axis_index("tx"), lax.axis_index("ty")
     has_prev, has_next = win > 0, win < nwin - 1
     right, left = lax.rem(tx + 1, ntx), lax.rem(tx + ntx - 1, ntx)
     lane = lax.broadcasted_iota(jnp.int32, (8, 128), 1)
-    axes = (("ty", nty, ty), ("tx", ntx, tx), ("win", nwin, win))
+    is_last = (win == nwin - 1) & has_prev
+    rounds = (
+        (tx, ntx, [{"tx": lax.rem(tx + j, ntx)} for j in range(1, ntx)]),
+        (ty * nwin + win, nty * nwin, [
+            {"ty": lax.rem(ty + j // nwin, nty), "win": lax.rem(win + j % nwin, nwin)}
+            for j in range(1, nty * nwin)]),
+    )
 
     brought = [
         pltpu.make_async_copy(src, dst, i_sem.at[i])
@@ -34,16 +40,16 @@
         copy.start()
 
     barrier = pltpu.get_barrier_semaphore()
-    for name, n, me in axes:
-        for j in range(1, n):
-            pl.semaphore_signal(barrier, inc=1, device_id={name: lax.rem(me + j, n)}, device_id_type=MESH)
+    for _, _, partners in rounds:
+        for partner in partners:
+            pl.semaphore_signal(barrier, inc=1, device_id=partner, device_id_type=MESH)
 
     @pl.when(win == nwin - 1)
     def _():
         foll[...] = jnp.zeros(foll.shape, jnp.float32)
         plin[...] = jnp.zeros(plin.shape, jnp.float32)
 
-    pl.semaphore_wait(barrier, (nty - 1) + (ntx - 1) + (nwin - 1))
+    pl.semaphore_wait(barrier, (ntx - 1) + (nty * nwin - 1))
 
     north_of, south_of = lax.rem(ty + 1, nty), lax.rem(ty + nty - 1, nty)
     to = ({"tx": left}, {"tx": right}, {"ty": south_of}, {"ty": north_of})
@@ -78,7 +84,12 @@
 
     @pl.when(has_prev)
     def _():
-        for c in range(nlev):
+        for c in range(2):
+            wcopy(0, c).start()
+
+    @pl.when(has_prev & has_next)
+    def _():
+        for c in range(2, nlev):
             wcopy(0, c).start()
 
     def loop(n, body):
@@ -245,15 +256,62 @@
             for g in range(groups) for p in range(nf)}
         for (p, g), y in done.items():
             back[c, p, span(g), :] = y
-
-        @pl.when(win == nwin - 1)
-        def _():
-            pls[c] = dual[0, :, c] + back[c]
-            if nwin > 1:
-                wcopy(1, c).start()
+        pls[c] = dual[0, :, c] + back[c]
+
+    def fold(x):
+        return jnp.sum(x.reshape(-1, 8, 128), axis=0)
+
+    def suffix(c):
+        @pl.when(has_next)
+        def _():
+            wcopy(1, c).wait_recv()
+            pls[c] = pls[c] + plin[c]
+
+        @pl.when(has_next & has_prev)
+        def _():
+            wcopy(1, c).start()
+
+        lam = dual[0, :, c]
+        new = pls[c]
+        base = mv[0, :, c] * (lam - new) + inc[0, :, c]
+        pxs[c] = base
+
+        @pl.when((win == 0) & has_next)
+        def _():
+            gout[c] = base - moved[c, :, pl.ds(PAD, rows), :]
+            wcopy(2, c).start()
+
+        wsum[...] = wsum[...] + fold(new * lam)
+
+    order = [(0, c) for c in range(nlev)] + [(1, c) for c in range(nlev)]
+
+    def follow(i):
+        @pl.when(is_last)
+        def _():
+            wcopy(*order[i]).wait_send()
+            wcopy(*order[i + 2]).start()
+
+    def diagonal(q):
+        for t in range(steps, -1, -1):
+            @pl.when((q >= t) & (q - t < nlev))
+            def _(t=t):
+                if t == 0:
+                    adjoint_first(q)
+                elif t < steps:
+                    adjoint(t - 1, q - t)
+                else:
+                    adjoint_last(q - t)
+
+        @pl.when(q > steps)
+        def _():
+            suffix(q - steps - 1)
+
+        for i in range(nlev - 2):
+            pl.when(q == 2 * i + 1)(lambda i=i: follow(i))
 
     for copy in brought:
         copy.wait()
+    wsum[...] = zero_tile
 
     def model(stage):
         now = lax.rem(stage + jnp.where(win == nwin - 1, 1, 0), 2)
@@ -261,18 +319,21 @@
         @pl.when(now == 0)
         def _():
             loop(nlev, forward_first)
-            loop(steps, lambda s: loop(nlev, lambda c: forward(s, c)))
+            follow(nlev - 1)
+
+            def forward_round(s):
+                loop(nlev, lambda c: forward(s, c))
+                for i in range(nlev - 2):
+                    pl.when(s == i)(lambda i=i: follow(nlev + i))
+
+            loop(steps, forward_round)
 
         @pl.when(now == 1)
         def _():
-            loop(nlev, adjoint_first)
-            loop(steps - 1, lambda t: loop(nlev, lambda c: adjoint(t, c)))
-            loop(nlev, adjoint_last)
+            loop(nlev + steps + 1, diagonal)
+            follow(nlev - 2)
 
     loop(2, model)
-
-    def fold(x):
-        return jnp.sum(x.reshape(-1, 8, 128), axis=0)
 
     def observe(c, carry):
         return tuple(
@@ -280,7 +341,7 @@
             for o in range(nobs))
 
     ends = lax.fori_loop(0, nlev, observe, tuple(jnp.zeros((rows, 128), jnp.float32) for _ in range(nobs)))
-    wv0, vv0 = zero_tile, zero_tile
+    wv0, vv0 = wsum[...], zero_tile
     for o in range(nobs):
         v = obs[0, o]
         pm = (ov[0, o] * v + ends[o]) / ov[0, o]
@@ -293,30 +354,6 @@
 
     vv = lax.fori_loop(0, nlev, squares, vv0)
 
-    def suffix(c, acc):
-        @pl.when(has_next)
-        def _():
-            wcopy(1, c).wait_recv()
-            pls[c] = dual[0, :, c] + back[c] + plin[c]
-
-        @pl.when(has_next & has_prev)
-        def _():
-            wcopy(1, c).start()
-
-        lam = dual[0, :, c]
-        new = pls[c]
-        base = mv[0, :, c] * (lam - new) + inc[0, :, c]
-        pxs[c] = base
-
-        @pl.when((win == 0) & has_next)
-        def _():
-            gout[c] = base - moved[c, :, pl.ds(PAD, rows), :]
-            wcopy(2, c).start()
-
-        return acc + fold(new * lam)
-
-    wv = lax.fori_loop(0, nlev, suffix, wv0)
-
     def prefix(c, acc):
         @pl.when(has_prev)
         def _():
@@ -330,7 +367,7 @@
 
         return acc + fold(pxs[c] * inc[0, :, c])
 
-    wv = lax.fori_loop(0, nlev, prefix, wv)
+    wv = lax.fori_loop(0, nlev, prefix, wv0)
 
     def total(x):
         return jnp.broadcast_to(jnp.sum(jnp.sum(x, axis=0, keepdims=True), axis=1, keepdims=True), (1, 128))
@@ -353,30 +390,28 @@
     uu = total(lax.fori_loop(0, nlev, residual, uu))
 
     at = 0
-    for index, (name, n, me) in enumerate(axes):
-        mine = red.at[at + me]
+    for me, n, partners in rounds:
         red[at + me, 0:1, :] = uu
         red[at + me, 1:2, :] = wv
         red[at + me, 2:3, :] = vv
-
-        def swap(j, name=name, n=n, me=me, at=at):
-            return pltpu.make_async_remote_copy(
+        swaps = [
+            pltpu.make_async_remote_copy(
                 src_ref=red.at[at + me], dst_ref=red.at[at + me],
                 send_sem=r_send.at[at + j], recv_sem=r_recv.at[at + j],
-                device_id={name: lax.rem(me + j, n)}, device_id_type=MESH)
-
-        for j in range(1, n):
-            swap(j).start()
-        for j in range(1, n):
-            swap(j).wait_recv()
+                device_id=partner, device_id_type=MESH)
+            for j, partner in enumerate(partners)]
+        for swap in swaps:
+            swap.start()
+        for swap in swaps:
+            swap.wait_recv()
         parts = [tuple(red[at + i, q:q + 1, :] for q in range(3)) for i in range(n)]
         wv = functools.reduce(lambda a, b: a + b, [q[1] for q in parts])
         vv = functools.reduce(lambda a, b: a + b, [q[2] for q in parts])
         h = ratio(wv, vv)
         uu = functools.reduce(
             lambda a, b: a + b, [q[0] + (ratio(q[1], q[2]) - h) * (ratio(q[1], q[2]) - h) * q[2] for q in parts])
-        for j in range(1, n):
-            swap(j).wait_send()
+        for swap in swaps:
+            swap.wait_send()
         at += n
 
     h = wv / vv
@@ -398,8 +433,13 @@
             src_ref=sbuf.at[kind], dst_ref=rbuf.at[kind], send_sem=h_send.at[kind],
             recv_sem=h_recv.at[kind, 0, 0], device_id=to[0], device_id_type=MESH).wait_send()
 
+    @pl.when(is_last)
+    def _():
+        for i in order[-2:]:
+            wcopy(*i).wait_send()
+
     def settle(c):
-        @pl.when(has_prev)
+        @pl.when(has_prev & has_next)
         def _():
             wcopy(0, c).wait_send()
             wcopy(1, c).wait_send()
@@ -415,13 +455,13 @@
     nwin, ntx, nty = (mesh.shape[a] for a in ("win", "tx", "ty"))
     _, nf, nlev, rows, cols = dual.shape
     nobs, steps = obs_dual.shape[1], trajectory.shape[1]
-    assert cols == 128 and rows % 8 == 0 and nf * rows // 4 <= 128 and nf <= 8
+    assert cols == 128 and rows % 8 == 0 and steps >= nlev - 2 >= 1 and nf * rows // 4 <= 128 and nf <= 8
     count = (2 * nf * nlev + nobs) * rows * cols * nwin * ntx * nty
     sizes = (nwin, ntx, nty, steps, nf, nlev, rows, nobs, float(count))
     vmem, smem = pl.BlockSpec(memory_space=pltpu.VMEM), pl.BlockSpec(memory_space=pltpu.SMEM)
     chunks = pltpu.VMEM((nlev, nf, rows, cols), jnp.float32)
     messages = pltpu.VMEM((2, steps, nlev, 4, 8, cols), jnp.float32)
-    n_red = nwin + ntx + nty
+    n_red = ntx + nty * nwin
     return pl.pallas_call(
         functools.partial(kernel, sizes),
         out_shape=(
@@ -444,6 +484,7 @@
             pltpu.VMEM((nobs, rows, cols), jnp.float32),
             messages, messages,
             pltpu.VMEM((n_red, 8, cols), jnp.float32),
+            pltpu.VMEM((8, cols), jnp.float32),
             pltpu.SemaphoreType.DMA((2,)),
             pltpu.SemaphoreType.DMA((2, steps, nlev)),
             pltpu.SemaphoreType.DMA((3, nlev)),

time: 58.9 us -> 62.8 us (1.066)
  Pallas kernels: 54.2 us -> 58.1 us
    pallas_call x1, Pallas kernels: 54.2 us -> 58.1 us  [per_device(): pl.pallas_call(functools.partial(kernel, sizes), out_shape=(jax.ShapeDtyp...]
where the time goes in v4:
time: 62.8 us; the launch traced here: 62.6 us
  Pallas kernels  58.1 us (93%)
  local copies, waits for them, and re-layouts  3.89 us (6%)
  between operations  0.66 us (1%)
    pallas_call x1, Pallas kernels, per_device(): pl.pallas_call(functools.partial(kernel, sizes), out_shape=(jax.ShapeDtyp...  58.1 us
    unnamed x10, local copies, waits for them, and re-layouts  3.89 us

profile of v4, /device:TPU:0, one launch (start us, length us, event | category | flops | bytes accessed | tf_op | source)
XLA Modules:
  0.0 62.6 jit_solution(8980409505784550431)
XLA Ops:
  0.6 58.1 %shard_map.111 = (f32[1,4,4,64,128]{4,3,2,1,0:T(8,128)}, f32[1,2,64,128]{3,2,1,0:T(8,128)}, f32[1,4,4,64,128]{4,3,2,1,0:T(8,128)}, f32[2]{0:T(128)}) custom-call(f32[1,4,4,64,128]{4,3,2,1,0:T(8,128)} %h_dual.1, f32[1,2,64,128]{3,2,1,0:T(8,128)} %h_obs.1, f32[1,4,4,64,128]{4,3,2,1,0:T(8,128)} %h_inc.1, f32[1,3,2,4,64,128]{5,4,3,2,1,0:T(8,128)} %h_traj.1, ...), custom_call_target="tpu_custom_call" | custom-call | tf_op jit(solution)/shard_map/pallas_call | solution.py:465
  58.7 0.0 copy-start.1
  58.7 0.0 copy-start
  58.8 1.9 %copy.16 = f32[1,4,4,64,128]{4,3,2,1,0:T(8,128)} copy(f32[1,4,4,64,128]{4,3,2,1,0:T(8,128)} %get-tuple-element.8) | data formatting | bytes 1048576
  60.7 0.0 copy-done.1
  60.7 0.6 %copy.17 = f32[1,2,64,128]{3,2,1,0:T(8,128)} copy(f32[1,2,64,128]{3,2,1,0:T(8,128)S(1)} %copy-done.1) | data formatting | bytes 131072
  61.3 0.0 copy-done
  61.3 0.0 copy-start.2
  61.3 0.8 %copy.18 = f32[1,4,4,64,128]{4,3,2,1,0:T(8,128)} copy(f32[1,4,4,64,128]{4,3,2,1,0:T(8,128)S(1)} %copy-done) | data formatting | bytes 1048576
  62.1 0.0 copy-done.2
  62.1 0.5 copy.19
Async XLA Ops:
  58.7 2.0 %copy-start.1 = (f32[1,2,64,128]{3,2,1,0:T(8,128)S(1)}, f32[1,2,64,128]{3,2,1,0:T(8,128)}, u32[]{:S(2)}) copy-start(f32[1,2,64,128]{3,2,1,0:T(8,128)} %get-tuple-element.9) | copy-start | bytes 196612
  58.7 2.6 %copy-start = (f32[1,4,4,64,128]{4,3,2,1,0:T(8,128)S(1)}, f32[1,4,4,64,128]{4,3,2,1,0:T(8,128)}, u32[]{:S(2)}) copy-start(f32[1,4,4,64,128]{4,3,2,1,0:T(8,128)} %get-tuple-element.10) | copy-start | bytes 1572868
  61.3 0.8 %copy-start.2 = (f32[2]{0:T(128)S(1)}, f32[2]{0:T(128)}, u32[]{:S(2)}) copy-start(f32[2]{0:T(128)} %get-tuple-element.11) | copy-start | bytes 28

commit v5 on v4

--- a/solution.py
+++ b/solution.py
@@ -85,11 +85,6 @@
     @pl.when(has_prev)
     def _():
         for c in range(2):
-            wcopy(0, c).start()
-
-    @pl.when(has_prev & has_next)
-    def _():
-        for c in range(2, nlev):
             wcopy(0, c).start()
 
     def loop(n, body):
@@ -258,6 +253,10 @@
             back[c, p, span(g), :] = y
         pls[c] = dual[0, :, c] + back[c]
 
+        @pl.when(is_last)
+        def _():
+            wcopy(1, c).start()
+
     def fold(x):
         return jnp.sum(x.reshape(-1, 8, 128), axis=0)
 
@@ -283,15 +282,21 @@
 
         wsum[...] = wsum[...] + fold(new * lam)
 
-    order = [(0, c) for c in range(nlev)] + [(1, c) for c in range(nlev)]
-
-    def follow(i):
-        @pl.when(is_last)
-        def _():
-            wcopy(*order[i]).wait_send()
-            wcopy(*order[i + 2]).start()
-
-    def diagonal(q):
+    def follow(c):
+        @pl.when(has_prev)
+        def _():
+            wcopy(0, c).wait_send()
+            wcopy(0, c + 2).start()
+
+    def slot_of_work(q):
+        @pl.when(q == 0)
+        def _():
+            loop(nlev, forward_first)
+
+        @pl.when((q >= 1) & (q <= steps))
+        def _():
+            loop(nlev, lambda c: forward(q - 1, c))
+
         for t in range(steps, -1, -1):
             @pl.when((q >= t) & (q - t < nlev))
             def _(t=t):
@@ -307,33 +312,13 @@
             suffix(q - steps - 1)
 
         for i in range(nlev - 2):
-            pl.when(q == 2 * i + 1)(lambda i=i: follow(i))
+            pl.when(q == i)(lambda i=i: follow(i))
 
     for copy in brought:
         copy.wait()
     wsum[...] = zero_tile
 
-    def model(stage):
-        now = lax.rem(stage + jnp.where(win == nwin - 1, 1, 0), 2)
-
-        @pl.when(now == 0)
-        def _():
-            loop(nlev, forward_first)
-            follow(nlev - 1)
-
-            def forward_round(s):
-                loop(nlev, lambda c: forward(s, c))
-                for i in range(nlev - 2):
-                    pl.when(s == i)(lambda i=i: follow(nlev + i))
-
-            loop(steps, forward_round)
-
-        @pl.when(now == 1)
-        def _():
-            loop(nlev + steps + 1, diagonal)
-            follow(nlev - 2)
-
-    loop(2, model)
+    loop(nlev + steps + 1, slot_of_work)
 
     def observe(c, carry):
         return tuple(
@@ -433,16 +418,14 @@
             src_ref=sbuf.at[kind], dst_ref=rbuf.at[kind], send_sem=h_send.at[kind],
             recv_sem=h_recv.at[kind, 0, 0], device_id=to[0], device_id_type=MESH).wait_send()
 
-    @pl.when(is_last)
-    def _():
-        for i in order[-2:]:
-            wcopy(*i).wait_send()
-
     def settle(c):
-        @pl.when(has_prev & has_next)
+        @pl.when(has_prev)
+        def _():
+            wcopy(1, c).wait_send()
+
+        @pl.when(has_prev & (c >= nlev - 2))
         def _():
             wcopy(0, c).wait_send()
-            wcopy(1, c).wait_send()
 
         @pl.when(has_next)
         def _():
@@ -455,7 +438,7 @@
     nwin, ntx, nty = (mesh.shape[a] for a in ("win", "tx", "ty"))
     _, nf, nlev, rows, cols = dual.shape
     nobs, steps = obs_dual.shape[1], trajectory.shape[1]
-    assert cols == 128 and rows % 8 == 0 and steps >= nlev - 2 >= 1 and nf * rows // 4 <= 128 and nf <= 8
+    assert cols == 128 and rows % 8 == 0 and nlev >= 2 and nf * rows // 4 <= 128 and nf <= 8
     count = (2 * nf * nlev + nobs) * rows * cols * nwin * ntx * nty
     sizes = (nwin, ntx, nty, steps, nf, nlev, rows, nobs, float(count))
     vmem, smem = pl.BlockSpec(memory_space=pltpu.VMEM), pl.BlockSpec(memory_space=pltpu.SMEM)

time: 62.8 us -> 55.7 us (0.89)
  Pallas kernels: 58.1 us -> 51 us
    pallas_call x1, Pallas kernels: 58.1 us -> 51 us  [per_device(): pl.pallas_call(functools.partial(kernel, sizes), out_shape=(jax.ShapeDtyp...]
where the time goes in v5:
time: 55.7 us; the launch traced here: 55.6 us
  Pallas kernels  51 us (92%)
  local copies, waits for them, and re-layouts  3.89 us (7%)
  between operations  0.66 us (1%)
    pallas_call x1, Pallas kernels, per_device(): pl.pallas_call(functools.partial(kernel, sizes), out_shape=(jax.ShapeDtyp...  51 us
    unnamed x10, local copies, waits for them, and re-layouts  3.89 us

profile of v5, /device:TPU:0, one launch (start us, length us, event | category | flops | bytes accessed | tf_op | source)
XLA Modules:
  0.0 55.6 jit_solution(14037927728904703634)
XLA Ops:
  0.6 51.0 %shard_map.111 = (f32[1,4,4,64,128]{4,3,2,1,0:T(8,128)}, f32[1,2,64,128]{3,2,1,0:T(8,128)}, f32[1,4,4,64,128]{4,3,2,1,0:T(8,128)}, f32[2]{0:T(128)}) custom-call(f32[1,4,4,64,128]{4,3,2,1,0:T(8,128)} %h_dual.1, f32[1,2,64,128]{3,2,1,0:T(8,128)} %h_obs.1, f32[1,4,4,64,128]{4,3,2,1,0:T(8,128)} %h_inc.1, f32[1,3,2,4,64,128]{5,4,3,2,1,0:T(8,128)} %h_traj.1, ...), custom_call_target="tpu_custom_call" | custom-call | tf_op jit(solution)/shard_map/pallas_call | solution.py:448
  51.7 0.0 copy-start.1
  51.7 0.0 copy-start
  51.7 1.9 %copy.16 = f32[1,4,4,64,128]{4,3,2,1,0:T(8,128)} copy(f32[1,4,4,64,128]{4,3,2,1,0:T(8,128)} %get-tuple-element.8) | data formatting | bytes 1048576
  53.6 0.0 copy-done.1
  53.6 0.6 %copy.17 = f32[1,2,64,128]{3,2,1,0:T(8,128)} copy(f32[1,2,64,128]{3,2,1,0:T(8,128)S(1)} %copy-done.1) | data formatting | bytes 131072
  54.3 0.0 copy-done
  54.3 0.0 copy-start.2
  54.3 0.8 %copy.18 = f32[1,4,4,64,128]{4,3,2,1,0:T(8,128)} copy(f32[1,4,4,64,128]{4,3,2,1,0:T(8,128)S(1)} %copy-done) | data formatting | bytes 1048576
  55.1 0.0 copy-done.2
  55.1 0.5 copy.19
Async XLA Ops:
  51.7 2.0 %copy-start.1 = (f32[1,2,64,128]{3,2,1,0:T(8,128)S(1)}, f32[1,2,64,128]{3,2,1,0:T(8,128)}, u32[]{:S(2)}) copy-start(f32[1,2,64,128]{3,2,1,0:T(8,128)} %get-tuple-element.9) | copy-start | bytes 196612
  51.7 2.6 %copy-start = (f32[1,4,4,64,128]{4,3,2,1,0:T(8,128)S(1)}, f32[1,4,4,64,128]{4,3,2,1,0:T(8,128)}, u32[]{:S(2)}) copy-start(f32[1,4,4,64,128]{4,3,2,1,0:T(8,128)} %get-tuple-element.10) | copy-start | bytes 1572868
  54.3 0.8 %copy-start.2 = (f32[2]{0:T(128)S(1)}, f32[2]{0:T(128)}, u32[]{:S(2)}) copy-start(f32[2]{0:T(128)} %get-tuple-element.11) | copy-start | bytes 28

commit v6 on v5

--- a/solution.py
+++ b/solution.py
@@ -282,11 +282,11 @@
 
         wsum[...] = wsum[...] + fold(new * lam)
 
-    def follow(c):
-        @pl.when(has_prev)
-        def _():
-            wcopy(0, c).wait_send()
-            wcopy(0, c + 2).start()
+    def begun(slot, body):
+        def one(i):
+            c = 2 * slot - 1 + i
+            pl.when((c >= 0) & (c < nlev))(lambda: body(c))
+        loop(2, one)
 
     def slot_of_work(q):
         @pl.when(q == 0)
@@ -297,28 +297,19 @@
         def _():
             loop(nlev, lambda c: forward(q - 1, c))
 
+        @pl.when(has_prev & (q + 2 < nlev))
+        def _():
+            wcopy(0, q + 2).start()
+
         for t in range(steps, -1, -1):
-            @pl.when((q >= t) & (q - t < nlev))
-            def _(t=t):
-                if t == 0:
-                    adjoint_first(q)
-                elif t < steps:
-                    adjoint(t - 1, q - t)
-                else:
-                    adjoint_last(q - t)
-
-        @pl.when(q > steps)
-        def _():
-            suffix(q - steps - 1)
-
-        for i in range(nlev - 2):
-            pl.when(q == i)(lambda i=i: follow(i))
+            begun(q - t, adjoint_first if t == 0 else adjoint_last if t == steps else functools.partial(adjoint, t - 1))
+        begun(q - steps - 1, suffix)
 
     for copy in brought:
         copy.wait()
     wsum[...] = zero_tile
 
-    loop(nlev + steps + 1, slot_of_work)
+    loop(nlev // 2 + steps + 2, slot_of_work)
 
     def observe(c, carry):
         return tuple(
@@ -421,11 +412,8 @@
     def settle(c):
         @pl.when(has_prev)
         def _():
+            wcopy(0, c).wait_send()
             wcopy(1, c).wait_send()
-
-        @pl.when(has_prev & (c >= nlev - 2))
-        def _():
-            wcopy(0, c).wait_send()
 
         @pl.when(has_next)
         def _():

time: 55.7 us -> 56.2 us (level)
  no operation moved by 1% of the time
where the time goes in v6:
time: 56.2 us; the launch traced here: 56 us
  Pallas kernels  51.5 us (92%)
  local copies, waits for them, and re-layouts  3.89 us (7%)
  between operations  0.66 us (1%)
    pallas_call x1, Pallas kernels, per_device(): pl.pallas_call(functools.partial(kernel, sizes), out_shape=(jax.ShapeDtyp...  51.5 us
    unnamed x10, local copies, waits for them, and re-layouts  3.89 us

profile of v6, /device:TPU:0, one launch (start us, length us, event | category | flops | bytes accessed | tf_op | source)
XLA Modules:
  0.0 56.0 jit_solution(9227058277357676836)
XLA Ops:
  0.6 51.5 %shard_map.111 = (f32[1,4,4,64,128]{4,3,2,1,0:T(8,128)}, f32[1,2,64,128]{3,2,1,0:T(8,128)}, f32[1,4,4,64,128]{4,3,2,1,0:T(8,128)}, f32[2]{0:T(128)}) custom-call(f32[1,4,4,64,128]{4,3,2,1,0:T(8,128)} %h_dual.1, f32[1,2,64,128]{3,2,1,0:T(8,128)} %h_obs.1, f32[1,4,4,64,128]{4,3,2,1,0:T(8,128)} %h_inc.1, f32[1,3,2,4,64,128]{5,4,3,2,1,0:T(8,128)} %h_traj.1, ...), custom_call_target="tpu_custom_call" | custom-call | tf_op jit(solution)/shard_map/pallas_call | solution.py:436
  52.1 0.0 copy-start.1
  52.1 0.0 copy-start
  52.1 1.9 %copy.16 = f32[1,4,4,64,128]{4,3,2,1,0:T(8,128)} copy(f32[1,4,4,64,128]{4,3,2,1,0:T(8,128)} %get-tuple-element.8) | data formatting | bytes 1048576
  54.1 0.0 copy-done.1
  54.1 0.6 %copy.17 = f32[1,2,64,128]{3,2,1,0:T(8,128)} copy(f32[1,2,64,128]{3,2,1,0:T(8,128)S(1)} %copy-done.1) | data formatting | bytes 131072
  54.7 0.0 copy-done
  54.7 0.0 copy-start.2
  54.7 0.8 %copy.18 = f32[1,4,4,64,128]{4,3,2,1,0:T(8,128)} copy(f32[1,4,4,64,128]{4,3,2,1,0:T(8,128)S(1)} %copy-done) | data formatting | bytes 1048576
  55.5 0.0 copy-done.2
  55.5 0.5 copy.19
Async XLA Ops:
  52.1 2.0 %copy-start.1 = (f32[1,2,64,128]{3,2,1,0:T(8,128)S(1)}, f32[1,2,64,128]{3,2,1,0:T(8,128)}, u32[]{:S(2)}) copy-start(f32[1,2,64,128]{3,2,1,0:T(8,128)} %get-tuple-element.9) | copy-start | bytes 196612
  52.1 2.6 %copy-start = (f32[1,4,4,64,128]{4,3,2,1,0:T(8,128)S(1)}, f32[1,4,4,64,128]{4,3,2,1,0:T(8,128)}, u32[]{:S(2)}) copy-start(f32[1,4,4,64,128]{4,3,2,1,0:T(8,128)} %get-tuple-element.10) | copy-start | bytes 1572868
  54.7 0.8 %copy-start.2 = (f32[2]{0:T(128)S(1)}, f32[2]{0:T(128)}, u32[]{:S(2)}) copy-start(f32[2]{0:T(128)} %get-tuple-element.11) | copy-start | bytes 28

commit v7 on v5

--- a/solution.py
+++ b/solution.py
@@ -289,10 +289,6 @@
             wcopy(0, c + 2).start()
 
     def slot_of_work(q):
-        @pl.when(q == 0)
-        def _():
-            loop(nlev, forward_first)
-
         @pl.when((q >= 1) & (q <= steps))
         def _():
             loop(nlev, lambda c: forward(q - 1, c))
@@ -314,7 +310,9 @@
         for i in range(nlev - 2):
             pl.when(q == i)(lambda i=i: follow(i))
 
-    for copy in brought:
+    brought[0].wait()
+    loop(nlev, forward_first)
+    for copy in brought[1:]:
         copy.wait()
     wsum[...] = zero_tile
 

time: 55.7 us -> 55.7 us (level)
  no operation moved by 1% of the time
where the time goes in v7:
time: 55.7 us; the launch traced here: 55.6 us
  Pallas kernels  51 us (92%)
  local copies, waits for them, and re-layouts  3.89 us (7%)
  between operations  0.66 us (1%)
    pallas_call x1, Pallas kernels, per_device(): pl.pallas_call(functools.partial(kernel, sizes), out_shape=(jax.ShapeDtyp...  51 us
    unnamed x10, local copies, waits for them, and re-layouts  3.89 us

profile of v7, /device:TPU:0, one launch (start us, length us, event | category | flops | bytes accessed | tf_op | source)
XLA Modules:
  0.0 55.6 jit_solution(4050778479072669473)
XLA Ops:
  0.6 51.0 %shard_map.111 = (f32[1,4,4,64,128]{4,3,2,1,0:T(8,128)}, f32[1,2,64,128]{3,2,1,0:T(8,128)}, f32[1,4,4,64,128]{4,3,2,1,0:T(8,128)}, f32[2]{0:T(128)}) custom-call(f32[1,4,4,64,128]{4,3,2,1,0:T(8,128)} %h_dual.1, f32[1,2,64,128]{3,2,1,0:T(8,128)} %h_obs.1, f32[1,4,4,64,128]{4,3,2,1,0:T(8,128)} %h_inc.1, f32[1,3,2,4,64,128]{5,4,3,2,1,0:T(8,128)} %h_traj.1, ...), custom_call_target="tpu_custom_call" | custom-call | tf_op jit(solution)/shard_map/pallas_call | solution.py:446
  51.7 0.0 copy-start.1
  51.7 0.0 copy-start
  51.7 1.9 %copy.16 = f32[1,4,4,64,128]{4,3,2,1,0:T(8,128)} copy(f32[1,4,4,64,128]{4,3,2,1,0:T(8,128)} %get-tuple-element.8) | data formatting | bytes 1048576
  53.6 0.0 copy-done.1
  53.6 0.6 %copy.17 = f32[1,2,64,128]{3,2,1,0:T(8,128)} copy(f32[1,2,64,128]{3,2,1,0:T(8,128)S(1)} %copy-done.1) | data formatting | bytes 131072
  54.3 0.0 copy-done
  54.3 0.0 copy-start.2
  54.3 0.8 %copy.18 = f32[1,4,4,64,128]{4,3,2,1,0:T(8,128)} copy(f32[1,4,4,64,128]{4,3,2,1,0:T(8,128)S(1)} %copy-done) | data formatting | bytes 1048576
  55.1 0.0 copy-done.2
  55.1 0.5 copy.19
Async XLA Ops:
  51.7 2.0 %copy-start.1 = (f32[1,2,64,128]{3,2,1,0:T(8,128)S(1)}, f32[1,2,64,128]{3,2,1,0:T(8,128)}, u32[]{:S(2)}) copy-start(f32[1,2,64,128]{3,2,1,0:T(8,128)} %get-tuple-element.9) | copy-start | bytes 196612
  51.7 2.6 %copy-start = (f32[1,4,4,64,128]{4,3,2,1,0:T(8,128)S(1)}, f32[1,4,4,64,128]{4,3,2,1,0:T(8,128)}, u32[]{:S(2)}) copy-start(f32[1,4,4,64,128]{4,3,2,1,0:T(8,128)} %get-tuple-element.10) | copy-start | bytes 1572868
  54.3 0.8 %copy-start.2 = (f32[2]{0:T(128)S(1)}, f32[2]{0:T(128)}, u32[]{:S(2)}) copy-start(f32[2]{0:T(128)} %get-tuple-element.11) | copy-start | bytes 28
